TPU v7x, 32 devices: a whole 2x2x4 slice. The times are simulated.
32 devices in a mesh: span: 8 (over z, x), mix: 4 (over y, core).
Axes of the slice: x: 2, y: 2, z: 4, core: 2. Of those that a mesh axis runs over, the one named last changes fastest.
Arguments:
- audio: float32 [131072], P(('mix', 'span')), parts along dimension 0, may hold values from -6 to 6
- w_enc: float32 [16, 256], replicated, may hold values from -1.5 to 1.5
- intra_query: bfloat16 [256, 256], replicated, may hold values from -8 to 8, as said below
- intra_kv: bfloat16 [256, 512], replicated, may hold values from -8 to 8, as said below
- intra_out: bfloat16 [256, 256], replicated, may hold values from -0.375 to 0.375
- intra_up: bfloat16 [256, 1024], replicated, may hold values from -0.375 to 0.375
- intra_down: bfloat16 [1024, 256], replicated, may hold values from -0.1875 to 0.1875
- inter_query: bfloat16 [256, 256], replicated, may hold values from -8 to 8, as said below
- inter_kv: bfloat16 [256, 512], replicated, may hold values from -8 to 8, as said below
- inter_out: bfloat16 [256, 256], replicated, may hold values from -0.375 to 0.375
- inter_up: bfloat16 [256, 1024], replicated, may hold values from -0.375 to 0.375
- inter_down: bfloat16 [1024, 256], replicated, may hold values from -0.1875 to 0.1875
- w_mask: bfloat16 [256, 512], replicated, may hold values from -0.375 to 0.375
Outputs:
- separated: bfloat16 [16384, 512], P(('mix', 'span')), parts along dimension 0
There are 4 independent parts, one for each index of `mix`. A program takes and returns all parts, laid end to end along the dimension named above; an argument that names none is the same for every part. Nothing has to cross between parts.
Inputs may be any that keep to these rules, and one draw needn't show every extreme that they name: `intra_query`: projection weights of the query. `intra_kv`: projection weights of keys and values. `inter_query`: projection weights of the query. `inter_kv`: projection weights of keys and values.
All inputs are finite; a program needn't handle non-finite values.
Results may differ from a plain program's by a relative error of at most 0.025.
Values may be sent and summed in bfloat16 or wider, within the bound.
A program may use at most 64 MiB of HBM per device.

v0:
```python
import math

import jax
import jax.numpy as jnp
from jax import lax
from jax.sharding import PartitionSpec as P

HEADS = 8
K = 256
HOP = 128
STRIDE = 8
SPK = 2


def shifted_2(block, axis, distance):
    devices = range(lax.axis_size(axis))
    route = [(i - distance, i) for i in devices if i - distance in devices]
    return lax.ppermute(block, axis, route)


def norm_rows(values):
    center = values - jnp.mean(values, axis=-1, keepdims=True)
    spread = jnp.mean(center * center, axis=-1, keepdims=True)
    return center * lax.rsqrt(spread + 1e-05)


def positions_table(count, width):
    place = jnp.arange(count, dtype=jnp.float32)[:, None]
    index = jnp.arange(width // 2, dtype=jnp.float32)[None, :]
    angle = place * jnp.exp(-math.log(10000.0) * 2.0 * index / width)
    return jnp.concatenate([jnp.sin(angle), jnp.cos(angle)], axis=1)


def matmul(rows, weight):
    shape = rows.shape
    flat = rows.reshape(-1, shape[-1])
    result = jnp.dot(flat, weight, preferred_element_type=jnp.float32)
    return result.reshape(shape[:-1] + (weight.shape[1],))


def attend_block(items):
    query_vectors, key_matrix_rows, value_matrix_rows = items
    score_scale = 1.0 / math.sqrt(query_vectors.shape[-1])
    logit_scores = (
        jnp.einsum(
            "blhd,bmhd->bhlm", query_vectors, key_matrix_rows, preferred_element_type=jnp.float32
        )
        * score_scale
    )
    logit_scores = logit_scores - jnp.max(logit_scores, axis=-1, keepdims=True)
    softmax_weights = jnp.exp(logit_scores)
    softmax_weights = (softmax_weights / jnp.sum(softmax_weights, axis=-1, keepdims=True)).astype(
        jnp.bfloat16
    )
    return jnp.einsum(
        "bhlm,bmhd->blhd", softmax_weights, value_matrix_rows, preferred_element_type=jnp.float32
    ).astype(jnp.bfloat16)


def layer(inputs, w_query, w_kv, w_out, w_up, w_down):
    batch, length, width = inputs.shape
    depth = width // HEADS
    group = math.gcd(batch, max(1, 1024 // length))
    blocks = batch // group
    normed = norm_rows(inputs.astype(jnp.float32)).astype(jnp.bfloat16)
    query_vectors = (
        matmul(normed, w_query).astype(jnp.bfloat16).reshape(blocks, group, length, HEADS, depth)
    )
    pair = matmul(normed, w_kv).astype(jnp.bfloat16)
    key_matrix_rows = pair[..., :width].reshape(blocks, group, length, HEADS, depth)
    value_matrix_rows = pair[..., width:].reshape(blocks, group, length, HEADS, depth)
    mixed = lax.map(attend_block, (query_vectors, key_matrix_rows, value_matrix_rows)).reshape(
        batch, length, width
    )
    middle_value = (inputs.astype(jnp.float32) + matmul(mixed, w_out)).astype(jnp.bfloat16)
    second_operand = norm_rows(middle_value.astype(jnp.float32)).astype(jnp.bfloat16)
    hidden = jax.nn.relu(matmul(second_operand, w_up)).astype(jnp.bfloat16)
    return (middle_value.astype(jnp.float32) + matmul(hidden, w_down)).astype(jnp.bfloat16)


def encode_rows(samples, w_enc):
    blocks = samples.reshape(-1, STRIDE)
    frames = jnp.concatenate([blocks[:-1], blocks[1:]], axis=1)
    result = jnp.dot(
        frames, w_enc, precision=lax.Precision.HIGHEST, preferred_element_type=jnp.float32
    )
    return jax.nn.relu(result).astype(jnp.bfloat16)


def body(
    audio,
    w_enc,
    intra_query,
    intra_kv,
    intra_out,
    intra_up,
    intra_down,
    inter_query,
    inter_kv,
    inter_out,
    inter_up,
    inter_down,
    w_mask,
):
    frame_count = audio.shape[0] // STRIDE
    width = w_enc.shape[1]
    local_spans = frame_count // HOP
    devices = lax.axis_size("span")
    extra = shifted_2(audio[: (HOP + 1) * STRIDE], "span", -1)
    padded = encode_rows(jnp.concatenate([audio, extra], axis=0), w_enc)
    enc = padded[:frame_count]
    spans = jnp.concatenate(
        [
            padded[:frame_count].reshape(local_spans, HOP, width),
            padded[HOP:].reshape(local_spans, HOP, width),
        ],
        axis=1,
    )
    start = (spans.astype(jnp.float32) + positions_table(K, width)[None]).astype(jnp.bfloat16)
    intra = layer(start, intra_query, intra_kv, intra_out, intra_up, intra_down)
    per_device = K // devices
    grouped = intra.reshape(local_spans, devices, per_device, width)
    gathered = lax.all_to_all(grouped, "span", split_axis=1, concat_axis=0, tiled=True)
    total = gathered.shape[0]
    plain = gathered[:, 0]
    shifted = (plain.astype(jnp.float32) + positions_table(total, width)[:, None, :]).astype(
        jnp.bfloat16
    )
    turned = jnp.transpose(shifted, (1, 0, 2))
    result = layer(turned, inter_query, inter_kv, inter_out, inter_up, inter_down)
    inter = jnp.transpose(result, (1, 0, 2))[:, None]
    back = lax.all_to_all(inter, "span", split_axis=0, concat_axis=1, tiled=True).reshape(
        local_spans, K, width
    )
    second_half = back[:, HOP:]
    carried = shifted_2(second_half[-1], "span", 1)
    earlier = jnp.concatenate([carried[None], second_half[:-1]], axis=0)
    summed = back[:, :HOP].astype(jnp.float32) + earlier.astype(jnp.float32)
    summed = summed.reshape(frame_count, width).astype(jnp.bfloat16)
    mask = jax.nn.relu(jnp.dot(summed, w_mask, preferred_element_type=jnp.float32))
    repeated = jnp.concatenate([enc] * SPK, axis=1).astype(jnp.float32)
    return (mask * repeated).astype(jnp.bfloat16)


def solution(mesh):
    placed = (P(("mix", "span")), P(), P(), P(), P(), P(), P(), P(), P(), P(), P(), P(), P())
    return jax.shard_map(
        body, mesh=mesh, in_specs=placed, out_specs=P(("mix", "span"), None), check_vma=False
    )
```

profile of v0, /device:TPU:0, one launch (start us, length us, event | category | flops | bytes accessed | tf_op | source)
XLA Modules:
  0.0 93.9 jit_solution(18077941980625146535)
XLA Ops:
  0.8 1.3 %collective-permute-start = (f32[1032]{0:T(1024)S(1)}, f32[1032]{0:T(1024)S(1)}, u32[]{:S(2)}, u32[]{:S(2)}) collective-permute-start(f32[1032]{0:T(1024)S(1)} %slice.62), channel_id=1, source_target_pairs={{4,0},{8,4},{12,8},{16,12},{20,16},{24,20},{28,24},{5,1},{9,5},{13... | collective-permute-start | bytes 12392 | tf_op jit(solution)/shard_map/ppermute | solution.py:18
  3.3 3.9 %collective-permute-done = f32[1032]{0:T(1024)S(1)} collective-permute-done((f32[1032]{0:T(1024)S(1)}, f32[1032]{0:T(1024)S(1)}, u32[]{:S(2)}, u32[]{:S(2)}) %collective-permute-start) | collective-permute-done | bytes 4160 | tf_op jit(solution)/shard_map/ppermute | solution.py:18
  8.0 1.5 %fusion.39 = bf16[640,256]{1,0:T(8,128)(2,1)S(1)} fusion(f32[16,256]{1,0:T(8,128)} %param.14, f32[640,8]{0,1:T(8,128)S(1)} %copy.53, f32[640,8]{0,1:T(8,128)S(1)} %copy.52), kind=kOutput, calls=%fused_computation.59 | convolution fusion | flops 31795200 | bytes 385024 | tf_op jit(solution)/shard_map/dot_general | solution.py:84
  11.8 5.1 %fusion.100 = (f32[4,8,256]{2,1,0:T(8,128)S(1)}, f32[4,8,256,256]{2,3,1,0:T(8,128)}) fusion(bf16[4,256,8,32]{1,3,2,0:T(8,128)(2,1)S(1)} %bitcast.131, bf16[4,256,8,32]{1,3,2,0:T(8,128)(2,1)S(1)} %bitcast.126), kind=kOutput, calls=%fused_computation.123 | convolution fusion | flops 140509440 | bytes 9469952 | tf_op jit(solution)/shard_map/while/body/eval_jaxpr/sub | solution.py:50
  16.9 4.3 %fusion.27 = bf16[4,8,32,256]{3,2,1,0:T(8,128)(2,1)S(1)} fusion(bf16[4,256,8,32]{1,3,2,0:T(8,128)(2,1)S(1)} %bitcast.127, f32[4,8,256,256]{2,3,1,0:T(8,128)} %get-tuple-element.52, f32[4,8,256]{2,1,0:T(8,128)S(1)} %get-tuple-element.51), kind=kOutput, calls=%fused_computation.44 | convolution fusion | flops 138674176 | bytes 9469952 | tf_op jit(solution)/shard_map/while/body/eval_jaxpr/bhlm,bmhd->blhd/dot_general | solution.py:55
  22.0 1.4 %fusion.26 = bf16[4,256,256]{2,1,0:T(8,128)(2,1)S(1)} fusion(bf16[4,256,256]{2,1,0:T(8,128)(2,1)S(1)} %get-tuple-element.54, bf16[1024,256]{1,0:T(8,128)(2,1)S(1)} %copy-done, bf16[256,1024]{1,0:T(8,128)(2,1)S(1)} %copy-done.2, f32[4,256]{1,0:T(4,128)S(1)} %add_rsqrt_fusion.2, f32[4,256]{1,0:T(4,128)S(1)} %broadcast_multiply_fusion.2), kind=kOutput, calls=%fused_computation.43 | convolution fusion | flops 1077673984 | bytes 2105344 | tf_op jit(solution)/shard_map/dot_general | solution.py:37
  23.5 0.8 copy.59
  24.3 6.2 %all-to-all-start = ((bf16[4,8,32,256]{3,2,0,1:T(8,128)(2,1)}), bf16[4,8,32,256]{3,2,0,1:T(8,128)(2,1)S(1)}, u32[]{:S(2)}, u32[]{:S(2)}) async-start(bf16[4,8,32,256]{3,2,0,1:T(8,128)(2,1)} %copy.59), calls=%async_computation | async-start | bytes 1048576 | tf_op jit(solution)/shard_map/all_to_all | solution.py:123
  30.6 13.2 %all-to-all-done = bf16[4,8,32,256]{3,2,0,1:T(8,128)(2,1)S(1)} async-done(((bf16[4,8,32,256]{3,2,0,1:T(8,128)(2,1)}), bf16[4,8,32,256]{3,2,0,1:T(8,128)(2,1)S(1)}, u32[]{:S(2)}, u32[]{:S(2)}) %all-to-all-start) | async-done | bytes 524320 | tf_op jit(solution)/shard_map/all_to_all | solution.py:123
  45.0 1.3 %convolution_convert_fusion.2 = bf16[32,32,256]{2,1,0:T(8,128)(2,1)} fusion(bf16[32,32,256]{2,0,1:T(8,128)(2,1)S(1)} %get-tuple-element.31, f32[32,32]{1,0:T(8,128)S(1)} %add_rsqrt_fusion.1, f32[32,32]{1,0:T(8,128)S(1)} %broadcast_multiply_fusion.1, bf16[256,256]{1,0:T(8,128)(2,1)S(1)} %copy-done.7), kind=kOutput, calls=%fused_computation.45 | convolution fusion | flops 135528448 | bytes 1187840 | tf_op jit(solution)/shard_map/dot_general | solution.py:37
  46.3 2.6 %squeeze.34 = bf16[32,32,8,32]{3,2,1,0:T(8,128)(2,1)S(1)} reshape(bf16[32,32,256]{2,1,0:T(8,128)(2,1)} %convolution_convert_fusion.2) | data formatting | bytes 1048576 | tf_op jit(solution)/shard_map/while/body/jit(dynamic_index_in_dim)/squeeze | solution.py:72
  49.0 1.4 %convolution_convert_fusion = bf16[32,32,512]{2,1,0:T(8,128)(2,1)S(1)} fusion(bf16[32,32,256]{2,0,1:T(8,128)(2,1)S(1)} %get-tuple-element.31, f32[32,32]{1,0:T(8,128)S(1)} %add_rsqrt_fusion.1, f32[32,32]{1,0:T(8,128)S(1)} %broadcast_multiply_fusion.1, bf16[256,512]{1,0:T(8,128)(2,1)} %param.21), kind=kOutput, calls=%fused_computation.29 | convolution fusion | flops 270008320 | bytes 1843200 | tf_op jit(solution)/shard_map/dot_general | solution.py:37
  50.4 1.1 %fusion.96 = (bf16[32,32,256]{2,1,0:T(8,128)(2,1)}, bf16[32,32,256]{2,1,0:T(8,128)(2,1)}) fusion(bf16[32,32,512]{2,1,0:T(8,128)(2,1)S(1)} %convolution_convert_fusion), kind=kLoop, calls=%fused_computation.119 | loop fusion | bytes 2097152 | tf_op jit(solution)/shard_map/slice | solution.py:70
  51.5 3.5 %squeeze.35 = bf16[32,32,8,32]{3,2,1,0:T(8,128)(2,1)} reshape(bf16[32,32,256]{2,1,0:T(8,128)(2,1)} %get-tuple-element.32) | data formatting | bytes 1048576 | tf_op jit(solution)/shard_map/while/body/jit(dynamic_index_in_dim)/squeeze | solution.py:72
  55.0 2.8 %fusion.11 = f32[32,8,32,32]{2,3,1,0:T(8,128)S(1)} fusion(bf16[32,32,8,32]{3,2,1,0:T(8,128)(2,1)} %squeeze.35, bf16[32,32,8,32]{3,2,1,0:T(8,128)(2,1)S(1)} %squeeze.34), kind=kOutput, calls=%fused_computation.15 | convolution fusion | flops 16777216 | bytes 2097152 | tf_op jit(solution)/shard_map/while/body/eval_jaxpr/blhd,bmhd->bhlm/dot_general | solution.py:45
  57.8 3.2 %fusion.101 = (f32[32,8,32]{2,1,0:T(8,128)S(1)}, f32[32,8,32,32]{2,3,1,0:T(8,128)}) fusion(f32[32,8,32,32]{2,3,1,0:T(8,128)S(1)} %fusion.11), kind=kOutput, calls=%fused_computation.124 | output fusion | flops 1048607 | bytes 2129920 | tf_op jit(solution)/shard_map/while/body/eval_jaxpr/sub | solution.py:50
  61.0 1.9 %copy.75 = bf16[32,32,256]{1,2,0:T(8,128)(2,1)S(1)} copy(bf16[32,32,256]{2,1,0:T(8,128)(2,1)} %get-tuple-element.33) | data formatting | bytes 1048576 | tf_op jit(solution)/shard_map/while/body/jit(dynamic_index_in_dim)/squeeze | solution.py:72
  63.0 2.9 %fusion.16 = bf16[32,8,32,32]{3,2,1,0:T(8,128)(2,1)S(1)} fusion(bf16[32,32,8,32]{1,3,2,0:T(8,128)(2,1)S(1)} %bitcast.120, f32[32,8,32,32]{2,3,1,0:T(8,128)} %get-tuple-element.56, f32[32,8,32]{2,1,0:T(8,128)S(1)} %get-tuple-element.55), kind=kOutput, calls=%fused_computation.20 | convolution fusion | flops 17563648 | bytes 2129920 | tf_op jit(solution)/shard_map/while/body/eval_jaxpr/bhlm,bmhd->blhd/dot_general | solution.py:55
  65.9 0.8 convert_reduce_fusion.2
  67.2 2.6 %fusion.38 = bf16[32,1,32,256]{3,0,2,1:T(8,128)(2,1)S(1)} fusion(f32[32,32,256]{2,1,0:T(8,128)S(1)} %get-tuple-element.57, bf16[32,32,256]{2,0,1:T(8,128)(2,1)S(1)} %get-tuple-element.31, bf16[32,32,256]{2,1,0:T(8,128)(2,1)S(1)} %get-tuple-element.24, bf16[1024,256]{1,0:T(8,128)(2,1)} %param.24, bf16[256,1024]{1,0:T(8,128)(2,1)} %param.23, ...), kind=kOutput, calls=%fused_computation.58 | convolution fusion | flops 1078460416 | bytes 3678208 | tf_op jit(solution)/shard_map/dot_general | solution.py:37
  70.1 17.2 %all_to_all.24 = bf16[32,1,32,256]{3,2,1,0:T(8,128)(2,1)S(1)} all-to-all(bf16[32,1,32,256]{3,2,1,0:T(8,128)(2,1)S(1)} %copy.66), channel_id=1, replica_groups=mesh['span'=8,'mix'=4] {'span'}, dimensions={0} | all-to-all | bytes 1048576 | tf_op jit(solution)/shard_map/all_to_all | solution.py:132
  87.4 3.4 %collective-permute-start.1 = (bf16[128,256]{1,0:T(8,128)(2,1)S(1)}, bf16[128,256]{1,0:T(8,128)(2,1)S(1)}, u32[]{:S(2)}, u32[]{:S(2)}) collective-permute-start(bf16[128,256]{1,0:T(8,128)(2,1)S(1)} %slice_bitcast_fusion), channel_id=1, source_target_pairs={{0,4},{4,8},{8,12},{12,16},{16,20},{20,24},{24,28},{1,5},{5,9},{9,... | collective-permute-start | bytes 196616 | tf_op jit(solution)/shard_map/ppermute | solution.py:18
  90.8 1.9 %collective-permute-done.1 = bf16[128,256]{1,0:T(8,128)(2,1)S(1)} collective-permute-done((bf16[128,256]{1,0:T(8,128)(2,1)S(1)}, bf16[128,256]{1,0:T(8,128)(2,1)S(1)}, u32[]{:S(2)}, u32[]{:S(2)}) %collective-permute-start.1) | collective-permute-done | bytes 65568 | tf_op jit(solution)/shard_map/ppermute | solution.py:18
  92.8 1.1 %fusion.28 = bf16[512,512]{1,0:T(8,128)(2,1)} fusion(bf16[512,256]{1,0:T(8,128)(2,1)S(1)} %bitcast.129, bf16[256,512]{1,0:T(8,128)(2,1)S(1)} %copy-done.4, bf16[512,256]{1,0:T(8,128)(2,1)S(1)} %get-tuple-element.42), kind=kOutput, calls=%fused_computation.47 | convolution fusion | flops 136052736 | bytes 1310720 | tf_op jit(solution)/shard_map/dot_general | solution.py:140
  (56 shorter events, 8.0 us)
Async XLA Ops:
  0.0 22.0 %copy-start = (bf16[1024,256]{1,0:T(8,128)(2,1)S(1)}, bf16[1024,256]{1,0:T(8,128)(2,1)}, u32[]{:S(2)}) copy-start(bf16[1024,256]{1,0:T(8,128)(2,1)} %param.19) | copy-start | bytes 1572868
  0.0 10.1 %copy-start.3 = (bf16[256,512]{1,0:T(8,128)(2,1)S(1)}, bf16[256,512]{1,0:T(8,128)(2,1)}, u32[]{:S(2)}) copy-start(bf16[256,512]{1,0:T(8,128)(2,1)} %param.16) | copy-start | bytes 786436
  0.8 6.5 %collective-permute-start = (f32[1032]{0:T(1024)S(1)}, f32[1032]{0:T(1024)S(1)}, u32[]{:S(2)}, u32[]{:S(2)}) collective-permute-start(f32[1032]{0:T(1024)S(1)} %slice.62), channel_id=1, source_target_pairs={{4,0},{8,4},{12,8},{16,12},{20,16},{24,20},{28,24},{5,1},{9,5},{13... | collective-permute-start | bytes 12392 | tf_op jit(solution)/shard_map/ppermute | solution.py:18
  9.4 1.5 %copy-start.5 = (bf16[256,256]{1,0:T(8,128)(2,1)S(1)}, bf16[256,256]{1,0:T(8,128)(2,1)}, u32[]{:S(2)}) copy-start(bf16[256,256]{1,0:T(8,128)(2,1)} %param.15) | copy-start | bytes 393220
  16.9 4.3 %copy-start.6 = (bf16[256,256]{1,0:T(8,128)(2,1)S(1)}, bf16[256,256]{1,0:T(8,128)(2,1)}, u32[]{:S(2)}) copy-start(bf16[256,256]{1,0:T(8,128)(2,1)} %param.17) | copy-start | bytes 393220
  16.9 5.2 %copy-start.2 = (bf16[256,1024]{1,0:T(8,128)(2,1)S(1)}, bf16[256,1024]{1,0:T(8,128)(2,1)}, u32[]{:S(2)}) copy-start(bf16[256,1024]{1,0:T(8,128)(2,1)} %param.18) | copy-start | bytes 1572868
  23.4 21.6 %copy-start.7 = (bf16[256,256]{1,0:T(8,128)(2,1)S(1)}, bf16[256,256]{1,0:T(8,128)(2,1)}, u32[]{:S(2)}) copy-start(bf16[256,256]{1,0:T(8,128)(2,1)} %param.20) | copy-start | bytes 393220
  24.3 19.6 %all-to-all-start = ((bf16[4,8,32,256]{3,2,0,1:T(8,128)(2,1)}), bf16[4,8,32,256]{3,2,0,1:T(8,128)(2,1)S(1)}, u32[]{:S(2)}, u32[]{:S(2)}) async-start(bf16[4,8,32,256]{3,2,0,1:T(8,128)(2,1)} %copy.59), calls=%async_computation | async-start | bytes 1048576 | tf_op jit(solution)/shard_map/all_to_all | solution.py:123
  63.0 2.9 %copy-start.1 = (bf16[256,256]{1,0:T(8,128)(2,1)S(1)}, bf16[256,256]{1,0:T(8,128)(2,1)}, u32[]{:S(2)}) copy-start(bf16[256,256]{1,0:T(8,128)(2,1)} %param.22) | copy-start | bytes 393220
  69.8 23.0 %copy-start.4 = (bf16[256,512]{1,0:T(8,128)(2,1)S(1)}, bf16[256,512]{1,0:T(8,128)(2,1)}, u32[]{:S(2)}) copy-start(bf16[256,512]{1,0:T(8,128)(2,1)} %param.25) | copy-start | bytes 786436
  87.4 5.3 %collective-permute-start.1 = (bf16[128,256]{1,0:T(8,128)(2,1)S(1)}, bf16[128,256]{1,0:T(8,128)(2,1)S(1)}, u32[]{:S(2)}, u32[]{:S(2)}) collective-permute-start(bf16[128,256]{1,0:T(8,128)(2,1)S(1)} %slice_bitcast_fusion), channel_id=1, source_target_pairs={{0,4},{4,8},{8,12},{12,16},{16,20},{20,24},{24,28},{1,5},{5,9},{9,... | collective-permute-start | bytes 196616 | tf_op jit(solution)/shard_map/ppermute | solution.py:18
where the time goes:
time: 94.5 us; the launch traced here: 93.9 us
  matrix products  26.8 us (28%)
  waiting for transfers between devices  19 us (20%)
  blocking collectives  17.2 us (18%)
  local copies, waits for them, and re-layouts  13.2 us (14%)
  starting transfers between devices  10.9 us (12%)
  other arithmetic  6.49 us (7%)
    all_to_all x1, blocking collectives, body(): lax.all_to_all(inter, 'span', split_axis=0, concat_axis=1, tiled=True)  17.2 us
    all_to_all x1, waiting for transfers between devices, body(): lax.all_to_all(grouped, 'span', split_axis=1, concat_axis=0, tiled=True)  13.2 us
    dot_general x8, matrix products, matmul(): result = jnp.dot(flat, weight, preferred_element_type=jnp.float32)  9.12 us
    squeeze x3, local copies, waits for them, and re-layouts, layer(): lax.map(attend_block, (query_vectors, key_matrix_rows, value_matrix_rows))  8.1 us
    dot_general x2, matrix products, attend_block(): jnp.einsum('bhlm,bmhd->blhd', softmax_weights, value_matrix_rows, preferr...  7.21 us
    all_to_all x1, starting transfers between devices, body(): lax.all_to_all(grouped, 'span', split_axis=1, concat_axis=0, tiled=True)  6.22 us
    ppermute x2, waiting for transfers between devices, shifted_2(): return lax.ppermute(block, axis, route)  5.76 us
    sub x1, matrix products, attend_block(): logit_scores = logit_scores - jnp.max(logit_scores, axis=-1, keepdims=True)  5.07 us
  transfers between devices with their start and end apart: 3, of which 3 were waited for; matrix products, arithmetic and copies ran while one was open for 1% of the time, Pallas kernels for 0%

commit v1 on v0

--- a/solution.py
+++ b/solution.py
@@ -1,8 +1,12 @@
+import functools
 import math
 
 import jax
 import jax.numpy as jnp
+import numpy as np
 from jax import lax
+from jax.experimental import pallas as pl
+from jax.experimental.pallas import tpu as pltpu
 from jax.sharding import PartitionSpec as P
 
 HEADS = 8
@@ -87,7 +91,7 @@
     return jax.nn.relu(result).astype(jnp.bfloat16)
 
 
-def body(
+def plain_body(
     audio,
     w_enc,
     intra_query,
@@ -142,6 +146,390 @@
     return (mask * repeated).astype(jnp.bfloat16)
 
 
+LANES = 128
+TILE = 16
+MESH = pl.DeviceIdType.MESH
+
+
+def position_values(count, width):
+    place = np.arange(count, dtype=np.float64)[:, None]
+    index = np.arange(width // 2, dtype=np.float64)[None, :]
+    angle = place * np.exp(-math.log(10000.0) * 2.0 * index / width)
+    return np.concatenate([np.sin(angle), np.cos(angle)], axis=1).astype(np.float32)
+
+
+def dot(left, right):
+    return jnp.dot(left, right, preferred_element_type=jnp.float32)
+
+
+def round_rows(values):
+    return values.astype(jnp.bfloat16).astype(jnp.float32)
+
+
+def strided(ref, first, count, stride):
+    picked = [ref[side, pl.ds(first, count, stride=stride), :] for side in range(ref.shape[0])]
+    return jnp.concatenate(picked, axis=1)
+
+
+def attend_rows(query, key, value, bias):
+    rows, width = query.shape
+    depth = width // HEADS
+    owner = lax.broadcasted_iota(jnp.int32, (1, width), 1) // depth
+    zero = jnp.zeros((), jnp.bfloat16)
+    total = None
+    for head in range(HEADS):
+        mine = owner == head
+        scores = lax.dot_general(
+            jnp.where(mine, query, zero),
+            key,
+            (((1,), (1,)), ((), ())),
+            preferred_element_type=jnp.float32,
+        )
+        if bias is not None:
+            scores = scores + bias
+        scores = scores - jnp.max(scores, axis=-1, keepdims=True)
+        weights = jnp.exp2(scores * (math.log2(math.e) / math.sqrt(depth)))
+        weights = weights * (1.0 / jnp.sum(weights, axis=-1, keepdims=True))
+        part = dot(weights.astype(jnp.bfloat16), jnp.where(mine, value, zero))
+        total = part if total is None else total + part
+    return total.astype(jnp.bfloat16)
+
+
+def layer_rows(rows, group, bias, w_query, w_kv, w_out, w_up, w_down):
+    width = rows.shape[1]
+    normed = norm_rows(rows).astype(jnp.bfloat16)
+    query = dot(normed, w_query[...]).astype(jnp.bfloat16)
+    pair = dot(normed, w_kv[...]).astype(jnp.bfloat16)
+    mixed = [
+        attend_rows(
+            query[at : at + group],
+            pair[at : at + group, :width],
+            pair[at : at + group, width:],
+            bias,
+        )
+        for at in range(0, rows.shape[0], group)
+    ]
+    mixed = mixed[0] if len(mixed) == 1 else jnp.concatenate(mixed, axis=0)
+    middle = round_rows(rows + dot(mixed, w_out[...]))
+    second = norm_rows(middle).astype(jnp.bfloat16)
+    hidden = jnp.maximum(dot(second, w_up[...]), 0.0).astype(jnp.bfloat16)
+    return middle + dot(hidden, w_down[...])
+
+
+def separator_kernel(
+    devices,
+    group,
+    audio,
+    w_enc,
+    table_span,
+    table_across,
+    bias,
+    intra_query,
+    intra_kv,
+    intra_out,
+    intra_up,
+    intra_down,
+    inter_query,
+    inter_kv,
+    inter_out,
+    inter_up,
+    inter_down,
+    enc_ref,
+    summed_ref,
+    samples,
+    frames,
+    sent,
+    taken,
+    across,
+    inter,
+    back,
+    got,
+    halo_send,
+    halo_recv,
+    out_send,
+    out_recv,
+    back_send,
+    back_recv,
+):
+    me = lax.axis_index("span")
+    width = w_enc.shape[1]
+    rows = audio.shape[0]
+    per_row = LANES // STRIDE
+    count = rows * per_row
+    spans = count // HOP
+    share = HOP // devices
+    total = spans * devices
+    chunks = back.shape[0]
+    part = share // chunks
+    halo_rows = samples.shape[0] - rows
+
+    barrier = pltpu.get_barrier_semaphore()
+    for step in range(1, devices):
+        other = lax.rem(me + step, devices)
+        pl.semaphore_signal(barrier, inc=1, device_id={"span": other}, device_id_type=MESH)
+    samples[:rows] = audio[...]
+    pl.semaphore_wait(barrier, devices - 1)
+
+    halo = pltpu.make_async_remote_copy(
+        src_ref=audio.at[pl.ds(0, halo_rows)],
+        dst_ref=samples.at[pl.ds(rows, halo_rows)],
+        send_sem=halo_send,
+        recv_sem=halo_recv,
+        device_id={"span": lax.rem(me + devices - 1, devices)},
+        device_id_type=MESH,
+    )
+
+    @pl.when(me > 0)
+    def _():
+        halo.start()
+
+    lane = lax.broadcasted_iota(jnp.int32, (1, LANES), 1)
+    slot = lax.broadcasted_iota(jnp.int32, (HOP, 1), 0) % per_row
+    mine = lane // STRIDE == slot
+    w_low = jnp.concatenate([w_enc[:STRIDE]] * per_row, axis=0)
+    w_high = jnp.concatenate([w_enc[STRIDE:]] * per_row, axis=0)
+    w_both = jnp.concatenate([w_low, w_high], axis=0)
+    step_rows = HOP // per_row
+
+    def encode(hop):
+        at = hop * step_rows
+        low = samples[pl.ds(at, step_rows), :]
+        turned = pltpu.roll(samples[pl.ds(at, 2 * step_rows), :], LANES - STRIDE, 1)
+        high = jnp.where(lane < LANES - STRIDE, turned[:step_rows], turned[1 : step_rows + 1])
+        spread = [
+            jnp.concatenate(
+                [jnp.broadcast_to(block[r : r + 1], (per_row, LANES)) for r in range(step_rows)],
+                axis=0,
+            )
+            for block in (low, high)
+        ]
+        picked = jnp.concatenate([jnp.where(mine, block, 0.0) for block in spread], axis=1)
+        result = jnp.dot(
+            picked, w_both, precision=lax.Precision.HIGHEST, preferred_element_type=jnp.float32
+        )
+        frames[pl.ds(hop * HOP, HOP), :] = jnp.maximum(result, 0.0).astype(jnp.bfloat16)
+
+    for hop in range(spans - 1):
+        encode(hop)
+
+    def send_out(index, step):
+        other = lax.rem(me + step, devices)
+        return pltpu.make_async_remote_copy(
+            src_ref=sent.at[index, :, pl.ds(pl.multiple_of(other * share, TILE), share), :],
+            dst_ref=taken.at[me * spans + index],
+            send_sem=out_send.at[index, step],
+            recv_sem=out_recv.at[index, step],
+            device_id={"span": other},
+            device_id_type=MESH,
+        )
+
+    def do_span(index, _):
+        @pl.when(index == spans - 2)
+        def _():
+            @pl.when(me < devices - 1)
+            def _():
+                halo.wait_recv()
+
+            @pl.when(me == devices - 1)
+            def _():
+                samples[rows:] = jnp.zeros((halo_rows, LANES), jnp.float32)
+
+            encode(spans - 1)
+            encode(spans)
+
+        at = pl.multiple_of(index * HOP, HOP)
+        start = round_rows(
+            frames[pl.ds(at, K), :].astype(jnp.float32) + table_span[...]
+        )
+        result = layer_rows(
+            start, K, None, intra_query, intra_kv, intra_out, intra_up, intra_down
+        ).astype(jnp.bfloat16)
+        sent[index] = result.reshape(K // HOP, HOP, width)
+        for step in range(1, devices):
+            send_out(index, step).start()
+        taken[me * spans + index] = sent[
+            index, :, pl.ds(pl.multiple_of(me * share, TILE), share), :
+        ]
+        return 0
+
+    lax.fori_loop(0, spans, do_span, 0)
+    enc_ref[...] = frames[:count]
+
+    owned = 2 * share
+
+    def place(index, source):
+        row = source * spans + index
+        block = taken[row].reshape(owned, width).astype(jnp.float32)
+        at = pl.multiple_of(row * owned, owned)
+        block = round_rows(block + table_across[pl.ds(row, 1), :])
+        for side in range(width // LANES):
+            across[side, pl.ds(at, owned), :] = block[:, side * LANES : (side + 1) * LANES]
+
+    def place_all(index, _):
+        place(index, me)
+        for step in range(1, devices):
+            send_out(index, step).wait_recv()
+            place(index, lax.rem(me + devices - step, devices))
+        return 0
+
+    lax.fori_loop(0, spans, place_all, 0)
+
+    def send_back(chunk, step):
+        other = lax.rem(me + step, devices)
+        size = spans * part
+        return pltpu.make_async_remote_copy(
+            src_ref=back.at[chunk, pl.ds(pl.multiple_of(other * size, TILE), size), :],
+            dst_ref=got.at[chunk, me],
+            send_sem=back_send.at[chunk, step],
+            recv_sem=back_recv.at[chunk, step],
+            device_id={"span": other},
+            device_id_type=MESH,
+        )
+
+    def do_chunk(chunk, _):
+        def do_half(half, _):
+            first = half * share + chunk * part
+            block = jnp.concatenate(
+                [strided(across, first + p, total, owned) for p in range(part)], axis=0
+            )
+            result = layer_rows(
+                block, group, bias[...], inter_query, inter_kv, inter_out, inter_up, inter_down
+            )
+            at = pl.multiple_of(first * total, part * total)
+            result = round_rows(result)
+            for side in range(width // LANES):
+                inter[side, pl.ds(at, part * total), :] = result[
+                    :, side * LANES : (side + 1) * LANES
+                ]
+            return 0
+
+        lax.fori_loop(0, 2, do_half, 0)
+        near = chunk * part * total
+        far = (share + chunk * part) * total
+        pieces = []
+        for span in range(total):
+            piece = strided(inter, near + span, part, total)
+            if span > 0:
+                piece = piece + strided(inter, far + span - 1, part, total)
+            pieces.append(piece)
+        back[chunk] = jnp.concatenate(pieces, axis=0).astype(jnp.bfloat16)
+        for step in range(1, devices):
+            send_back(chunk, step).start()
+        size = spans * part
+        got[chunk, me] = back[chunk, pl.ds(pl.multiple_of(me * size, TILE), size), :]
+        return 0
+
+    lax.fori_loop(0, chunks, do_chunk, 0)
+
+    def collect(source):
+        pieces = [
+            got[chunk, source].astype(jnp.float32).reshape(spans, part, width)
+            for chunk in range(chunks)
+        ]
+        at = pl.multiple_of(source * share, TILE)
+        summed_ref[:, pl.ds(at, share), :] = jnp.concatenate(pieces, axis=1).astype(jnp.bfloat16)
+
+    collect(me)
+    for step in range(1, devices):
+        for chunk in range(chunks):
+            send_back(chunk, step).wait_recv()
+        collect(lax.rem(me + devices - step, devices))
+
+    @pl.when(me > 0)
+    def _():
+        halo.wait_send()
+
+    def drain_out(index, _):
+        for step in range(1, devices):
+            send_out(index, step).wait_send()
+        return 0
+
+    def drain_back(chunk, _):
+        for step in range(1, devices):
+            send_back(chunk, step).wait_send()
+        return 0
+
+    lax.fori_loop(0, spans, drain_out, 0)
+    lax.fori_loop(0, chunks, drain_back, 0)
+
+
+def kernel_body(devices, audio, w_enc, *weights):
+    *layers, w_mask = weights
+    width = w_enc.shape[1]
+    rows = audio.shape[0] // LANES
+    count = audio.shape[0] // STRIDE
+    spans = count // HOP
+    total = spans * devices
+    share = HOP // devices
+    chunks = 2
+    part = share // chunks
+    group = LANES
+    halo_rows = 2 * HOP * STRIDE // LANES
+    kind = np.arange(group) // total
+    bias = np.where(kind[:, None] == kind[None, :], 0.0, -1e30).astype(np.float32)
+    operands = (
+        audio.reshape(rows, LANES),
+        w_enc,
+        position_values(K, width),
+        position_values(total, width),
+        bias,
+        *layers,
+    )
+    vmem = pl.BlockSpec(memory_space=pltpu.VMEM)
+    dma = pltpu.SemaphoreType.DMA
+    enc, summed = pl.pallas_call(
+        functools.partial(separator_kernel, devices, group),
+        out_shape=[
+            jax.ShapeDtypeStruct((count, width), jnp.bfloat16),
+            jax.ShapeDtypeStruct((spans, HOP, width), jnp.bfloat16),
+        ],
+        in_specs=[vmem] * len(operands),
+        out_specs=[vmem] * 2,
+        scratch_shapes=[
+            pltpu.VMEM((rows + halo_rows, LANES), jnp.float32),
+            pltpu.VMEM((count + HOP, width), jnp.bfloat16),
+            pltpu.VMEM((spans, K // HOP, HOP, width), jnp.bfloat16),
+            pltpu.VMEM((total, K // HOP, share, width), jnp.bfloat16),
+            pltpu.VMEM((width // LANES, total * 2 * share, LANES), jnp.float32),
+            pltpu.VMEM((width // LANES, total * 2 * share, LANES), jnp.float32),
+            pltpu.VMEM((chunks, total * part, width), jnp.bfloat16),
+            pltpu.VMEM((chunks, devices, spans * part, width), jnp.bfloat16),
+            dma,
+            dma,
+            dma((spans, devices)),
+            dma((spans, devices)),
+            dma((chunks, devices)),
+            dma((chunks, devices)),
+        ],
+        compiler_params=pltpu.CompilerParams(
+            collective_id=0, has_side_effects=True, vmem_limit_bytes=40 * 2**20
+        ),
+    )(*operands)
+    summed = summed.reshape(count, width)
+    mask = jax.nn.relu(jnp.dot(summed, w_mask, preferred_element_type=jnp.float32))
+    repeated = jnp.concatenate([enc] * SPK, axis=1).astype(jnp.float32)
+    return (mask * repeated).astype(jnp.bfloat16)
+
+
+def fits_kernel(devices, count):
+    spans = count // HOP
+    share = HOP // devices
+    return (
+        HOP % devices == 0
+        and share % TILE == 0
+        and LANES % (spans * devices) == 0
+        and spans >= 3
+        and devices > 1
+    )
+
+
+def body(audio, w_enc, *weights):
+    devices = lax.axis_size("span")
+    if fits_kernel(devices, audio.shape[0] // STRIDE):
+        return kernel_body(devices, audio, w_enc, *weights)
+    return plain_body(audio, w_enc, *weights)
+
+
 def solution(mesh):
     placed = (P(("mix", "span")), P(), P(), P(), P(), P(), P(), P(), P(), P(), P(), P(), P())
     return jax.shard_map(

time: 94.5 us -> 55 us (0.58)
  Pallas kernels: 0 us -> 39.5 us
  matrix products: 26.8 us -> 1.1 us
  waiting for transfers between devices: 19 us -> 0 us
  blocking collectives: 17.2 us -> 0 us
  starting transfers between devices: 10.9 us -> 0 us
  other arithmetic: 6.49 us -> 0 us
    pallas_call x0 -> x1, Pallas kernels: none -> 39.5 us  [kernel_body(): pl.pallas_call(functools.partial(separator_kernel, devices, group), out_s...]
    dot_general x13 -> x1, matrix products: 21.7 us -> 1.1 us  [kernel_body(): jnp.dot(summed, w_mask, preferred_element_type=jnp.float32)]
    all_to_all x1 -> x0, blocking collectives: 17.2 us -> none  [body(): lax.all_to_all(inter, 'span', split_axis=0, concat_axis=1, tiled=True)]
    all_to_all x1 -> x0, waiting for transfers between devices: 13.2 us -> none  [body(): lax.all_to_all(grouped, 'span', split_axis=1, concat_axis=0, tiled=True)]
    unnamed x17 -> x32, local copies, waits for them, and re-layouts: 0.77 us -> 13.7 us
    squeeze x4 -> x0, local copies, waits for them, and re-layouts: 8.11 us -> none  [the longest x3 8.1 us: layer(): lax.map(attend_block, (query_vectors, key_matrix_rows, value_matrix_rows))]
    all_to_all x1 -> x0, starting transfers between devices: 6.22 us -> none  [body(): lax.all_to_all(grouped, 'span', split_axis=1, concat_axis=0, tiled=True)]
    ppermute x2 -> x0, waiting for transfers between devices: 5.76 us -> none  [shifted_2(): return lax.ppermute(block, axis, route)]
  transfers between devices with their start and end apart: 3 -> 0, of which waited for: 3 -> 0; matrix products, arithmetic and copies ran while one was open for 1% -> 0% of each run, Pallas kernels for 0% -> 0%
where the time goes in v1:
time: 55 us; the launch traced here: 54.3 us
  Pallas kernels  39.5 us (72%)
  local copies, waits for them, and re-layouts  13.7 us (25%)
  matrix products  1.1 us (2%)
    pallas_call x1, Pallas kernels, kernel_body(): pl.pallas_call(functools.partial(separator_kernel, devices, group), out_s...  39.5 us
    unnamed x32, local copies, waits for them, and re-layouts  13.7 us

profile of v1, /device:TPU:0, one launch (start us, length us, event | category | flops | bytes accessed | tf_op | source)
XLA Modules:
  0.0 54.3 jit_solution(670044956662321978)
XLA Ops:
  0.0 0.0 copy-start
  0.0 0.0 copy-start.1
  0.0 1.1 %copy-done.1 = bf16[256,1024]{1,0:T(8,128)(2,1)S(1)} copy-done((bf16[256,1024]{1,0:T(8,128)(2,1)S(1)}, bf16[256,1024]{1,0:T(8,128)(2,1)}, u32[]{:S(2)}) %copy-start.1) | copy-done | bytes 524312
  1.1 0.0 copy-start.2
  1.1 1.0 %copy-done.2 = bf16[1024,256]{1,0:T(8,128)(2,1)S(1)} copy-done((bf16[1024,256]{1,0:T(8,128)(2,1)S(1)}, bf16[1024,256]{1,0:T(8,128)(2,1)}, u32[]{:S(2)}) %copy-start.2) | copy-done | bytes 524312
  2.1 0.0 copy-start.3
  2.1 1.0 %copy-done.3 = bf16[256,1024]{1,0:T(8,128)(2,1)S(1)} copy-done((bf16[256,1024]{1,0:T(8,128)(2,1)S(1)}, bf16[256,1024]{1,0:T(8,128)(2,1)}, u32[]{:S(2)}) %copy-start.3) | copy-done | bytes 524312
  3.2 0.0 copy-start.4
  3.2 1.0 %copy-done.4 = bf16[1024,256]{1,0:T(8,128)(2,1)S(1)} copy-done((bf16[1024,256]{1,0:T(8,128)(2,1)S(1)}, bf16[1024,256]{1,0:T(8,128)(2,1)}, u32[]{:S(2)}) %copy-start.4) | copy-done | bytes 524312
  4.2 0.0 copy-start.5
  4.2 0.9 %copy-done.5 = bf16[256,512]{1,0:T(8,128)(2,1)S(1)} copy-done((bf16[256,512]{1,0:T(8,128)(2,1)S(1)}, bf16[256,512]{1,0:T(8,128)(2,1)}, u32[]{:S(2)}) %copy-start.5) | copy-done | bytes 262168
  5.2 0.9 %copy-done.6 = bf16[256,512]{1,0:T(8,128)(2,1)S(1)} copy-done((bf16[256,512]{1,0:T(8,128)(2,1)S(1)}, bf16[256,512]{1,0:T(8,128)(2,1)}, u32[]{:S(2)}) %copy-start.6) | copy-done | bytes 262168
  6.1 0.9 %copy-done.7 = f32[256,256]{1,0:T(8,128)S(1)} copy-done((f32[256,256]{1,0:T(8,128)S(1)}, f32[256,256]{1,0:T(8,128)}, u32[]{:S(2)}) %copy-start.7) | copy-done | bytes 262168
  7.1 0.9 %copy-done.8 = bf16[256,256]{1,0:T(8,128)(2,1)S(1)} copy-done((bf16[256,256]{1,0:T(8,128)(2,1)S(1)}, bf16[256,256]{1,0:T(8,128)(2,1)}, u32[]{:S(2)}) %copy-start.8) | copy-done | bytes 131096
  8.0 0.9 %copy-done.9 = bf16[256,256]{1,0:T(8,128)(2,1)S(1)} copy-done((bf16[256,256]{1,0:T(8,128)(2,1)S(1)}, bf16[256,256]{1,0:T(8,128)(2,1)}, u32[]{:S(2)}) %copy-start.9) | copy-done | bytes 131096
  8.9 0.9 %copy-done.10 = bf16[256,256]{1,0:T(8,128)(2,1)S(1)} copy-done((bf16[256,256]{1,0:T(8,128)(2,1)S(1)}, bf16[256,256]{1,0:T(8,128)(2,1)}, u32[]{:S(2)}) %copy-start.10) | copy-done | bytes 131096
  9.8 0.9 %copy-done.11 = bf16[256,256]{1,0:T(8,128)(2,1)S(1)} copy-done((bf16[256,256]{1,0:T(8,128)(2,1)S(1)}, bf16[256,256]{1,0:T(8,128)(2,1)}, u32[]{:S(2)}) %copy-start.11) | copy-done | bytes 131096
  10.7 0.8 %copy-done.12 = f32[128,128]{1,0:T(8,128)S(1)} copy-done((f32[128,128]{1,0:T(8,128)S(1)}, f32[128,128]{1,0:T(8,128)}, u32[]{:S(2)}) %copy-start.12) | copy-done | bytes 65560
  11.5 0.8 %copy-done.13 = f32[32,256]{1,0:T(8,128)S(1)} copy-done((f32[32,256]{1,0:T(8,128)S(1)}, f32[32,256]{1,0:T(8,128)}, u32[]{:S(2)}) %copy-start.13) | copy-done | bytes 32792
  12.3 0.7 %copy-done.14 = f32[4096]{0:T(1024)S(1)} copy-done((f32[4096]{0:T(1024)S(1)}, f32[4096]{0:T(1024)}, u32[]{:S(2)}) %copy-start.14) | copy-done | bytes 16408
  13.0 0.7 %copy-done.15 = f32[16,256]{1,0:T(8,128)S(1)} copy-done((f32[16,256]{1,0:T(8,128)S(1)}, f32[16,256]{1,0:T(8,128)}, u32[]{:S(2)}) %copy-start.15) | copy-done | bytes 16408
  13.7 39.5 %shard_map.154 = (bf16[512,256]{1,0:T(8,128)(2,1)S(1)}, bf16[4,128,256]{2,1,0:T(8,128)(2,1)S(1)}) custom-call(f32[32,128]{1,0:T(8,128)S(1)} %bitcast.4, f32[16,256]{1,0:T(8,128)S(1)} %copy-done.15, f32[256,256]{1,0:T(8,128)S(1)} %copy-done.7, f32[32,256]{1,0:T(8,128)S(1)} %copy-done.13, f32[128,128]{1,0:T(8,128)S(1)} %copy-done.12, ...), custom_call_target="tpu_custom_call" | custom-call | tf_op jit(solution)/shard_map/pallas_call | solution.py:480
  53.2 0.0 copy-done
  53.2 1.1 %fusion.1 = bf16[512,512]{1,0:T(8,128)(2,1)} fusion(bf16[512,256]{1,0:T(8,128)(2,1)S(1)} %bitcast.5, bf16[256,512]{1,0:T(8,128)(2,1)S(1)} %copy-done, bf16[512,256]{1,0:T(8,128)(2,1)S(1)} %get-tuple-element.8), kind=kOutput, calls=%fused_computation.2 | convolution fusion | flops 136052736 | bytes 1310720 | tf_op jit(solution)/shard_map/dot_general | solution.py:509
  (10 shorter events, 0.0 us)
Async XLA Ops:
  0.0 53.2 %copy-start = (bf16[256,512]{1,0:T(8,128)(2,1)S(1)}, bf16[256,512]{1,0:T(8,128)(2,1)}, u32[]{:S(2)}) copy-start(bf16[256,512]{1,0:T(8,128)(2,1)} %param.28) | copy-start | bytes 786436
  0.0 1.1 %copy-start.1 = (bf16[256,1024]{1,0:T(8,128)(2,1)S(1)}, bf16[256,1024]{1,0:T(8,128)(2,1)}, u32[]{:S(2)}) copy-start(bf16[256,1024]{1,0:T(8,128)(2,1)} %intra_up.1) | copy-start | bytes 1572868
  1.1 1.0 %copy-start.2 = (bf16[1024,256]{1,0:T(8,128)(2,1)S(1)}, bf16[1024,256]{1,0:T(8,128)(2,1)}, u32[]{:S(2)}) copy-start(bf16[1024,256]{1,0:T(8,128)(2,1)} %intra_down.1) | copy-start | bytes 1572868
  2.1 1.0 %copy-start.3 = (bf16[256,1024]{1,0:T(8,128)(2,1)S(1)}, bf16[256,1024]{1,0:T(8,128)(2,1)}, u32[]{:S(2)}) copy-start(bf16[256,1024]{1,0:T(8,128)(2,1)} %inter_up.1) | copy-start | bytes 1572868
  3.2 1.0 %copy-start.4 = (bf16[1024,256]{1,0:T(8,128)(2,1)S(1)}, bf16[1024,256]{1,0:T(8,128)(2,1)}, u32[]{:S(2)}) copy-start(bf16[1024,256]{1,0:T(8,128)(2,1)} %inter_down.1) | copy-start | bytes 1572868
  4.2 0.9 %copy-start.5 = (bf16[256,512]{1,0:T(8,128)(2,1)S(1)}, bf16[256,512]{1,0:T(8,128)(2,1)}, u32[]{:S(2)}) copy-start(bf16[256,512]{1,0:T(8,128)(2,1)} %intra_kv.1) | copy-start | bytes 786436
  5.2 0.9 %copy-start.6 = (bf16[256,512]{1,0:T(8,128)(2,1)S(1)}, bf16[256,512]{1,0:T(8,128)(2,1)}, u32[]{:S(2)}) copy-start(bf16[256,512]{1,0:T(8,128)(2,1)} %inter_kv.1) | copy-start | bytes 786436
  6.1 0.9 %copy-start.7 = (f32[256,256]{1,0:T(8,128)S(1)}, f32[256,256]{1,0:T(8,128)}, u32[]{:S(2)}) copy-start(f32[256,256]{1,0:T(8,128)} %constant.9.clone.table_span) | copy-start | bytes 786436
  7.1 0.9 %copy-start.8 = (bf16[256,256]{1,0:T(8,128)(2,1)S(1)}, bf16[256,256]{1,0:T(8,128)(2,1)}, u32[]{:S(2)}) copy-start(bf16[256,256]{1,0:T(8,128)(2,1)} %intra_query.1) | copy-start | bytes 393220
  8.0 0.9 %copy-start.9 = (bf16[256,256]{1,0:T(8,128)(2,1)S(1)}, bf16[256,256]{1,0:T(8,128)(2,1)}, u32[]{:S(2)}) copy-start(bf16[256,256]{1,0:T(8,128)(2,1)} %intra_out.1) | copy-start | bytes 393220
  8.9 0.9 %copy-start.10 = (bf16[256,256]{1,0:T(8,128)(2,1)S(1)}, bf16[256,256]{1,0:T(8,128)(2,1)}, u32[]{:S(2)}) copy-start(bf16[256,256]{1,0:T(8,128)(2,1)} %inter_query.1) | copy-start | bytes 393220
  9.8 0.9 %copy-start.11 = (bf16[256,256]{1,0:T(8,128)(2,1)S(1)}, bf16[256,256]{1,0:T(8,128)(2,1)}, u32[]{:S(2)}) copy-start(bf16[256,256]{1,0:T(8,128)(2,1)} %inter_out.1) | copy-start | bytes 393220
  10.7 0.8 %copy-start.12 = (f32[128,128]{1,0:T(8,128)S(1)}, f32[128,128]{1,0:T(8,128)}, u32[]{:S(2)}) copy-start(f32[128,128]{1,0:T(8,128)} %constant.11.clone.bias) | copy-start | bytes 196612
  11.5 0.8 %copy-start.13 = (f32[32,256]{1,0:T(8,128)S(1)}, f32[32,256]{1,0:T(8,128)}, u32[]{:S(2)}) copy-start(f32[32,256]{1,0:T(8,128)} %constant.10.clone.table_across) | copy-start | bytes 98308
  12.3 0.7 %copy-start.14 = (f32[4096]{0:T(1024)S(1)}, f32[4096]{0:T(1024)}, u32[]{:S(2)}) copy-start(f32[4096]{0:T(1024)} %param.16) | copy-start | bytes 49156
  13.0 0.7 %copy-start.15 = (f32[16,256]{1,0:T(8,128)S(1)}, f32[16,256]{1,0:T(8,128)}, u32[]{:S(2)}) copy-start(f32[16,256]{1,0:T(8,128)} %w_enc.1) | copy-start | bytes 49156

commit v2 on v1

--- a/solution.py
+++ b/solution.py
@@ -148,6 +148,7 @@
 
 LANES = 128
 TILE = 16
+OPERANDS = 14
 MESH = pl.DeviceIdType.MESH
 
 
@@ -174,31 +175,47 @@
 def attend_rows(query, key, value, bias):
     rows, width = query.shape
     depth = width // HEADS
-    owner = lax.broadcasted_iota(jnp.int32, (1, width), 1) // depth
+    owner = lax.broadcasted_iota(jnp.int32, (1, LANES), 1) // depth
     zero = jnp.zeros((), jnp.bfloat16)
-    total = None
-    for head in range(HEADS):
-        mine = owner == head
+    ones = jnp.ones((rows, LANES), jnp.bfloat16)
+    heads = LANES // depth
+    sides = []
+    for at in range(0, width, LANES):
+        side_query, side_key, side_value = (
+            block[:, at : at + LANES] for block in (query, key, value)
+        )
         scores = lax.dot_general(
-            jnp.where(mine, query, zero),
-            key,
+            jnp.concatenate(
+                [jnp.where(owner == head, side_query, zero) for head in range(heads)], axis=0
+            ),
+            side_key,
             (((1,), (1,)), ((), ())),
             preferred_element_type=jnp.float32,
         )
-        if bias is not None:
-            scores = scores + bias
-        scores = scores - jnp.max(scores, axis=-1, keepdims=True)
-        weights = jnp.exp2(scores * (math.log2(math.e) / math.sqrt(depth)))
-        weights = weights * (1.0 / jnp.sum(weights, axis=-1, keepdims=True))
-        part = dot(weights.astype(jnp.bfloat16), jnp.where(mine, value, zero))
-        total = part if total is None else total + part
-    return total.astype(jnp.bfloat16)
+        weights = []
+        values = []
+        for head in range(heads):
+            part = scores[head * rows : (head + 1) * rows]
+            if bias is not None:
+                part = part + bias
+            part = part - jnp.max(part, axis=-1, keepdims=True)
+            weights.append(jnp.exp2(part.astype(jnp.bfloat16)))
+            mine = owner == head
+            values.append(
+                jnp.concatenate(
+                    [jnp.where(mine, side_value, zero), jnp.where(mine, ones, zero)], axis=1
+                )
+            )
+        result = dot(jnp.concatenate(weights, axis=1), jnp.concatenate(values, axis=0))
+        sides.append(result[:, :LANES] / result[:, LANES:])
+    return jnp.concatenate(sides, axis=1).astype(jnp.bfloat16)
 
 
 def layer_rows(rows, group, bias, w_query, w_kv, w_out, w_up, w_down):
     width = rows.shape[1]
     normed = norm_rows(rows).astype(jnp.bfloat16)
-    query = dot(normed, w_query[...]).astype(jnp.bfloat16)
+    scale = math.log2(math.e) / math.sqrt(width // HEADS)
+    query = (dot(normed, w_query[...]) * scale).astype(jnp.bfloat16)
     pair = dot(normed, w_kv[...]).astype(jnp.bfloat16)
     mixed = [
         attend_rows(
@@ -219,24 +236,15 @@
 def separator_kernel(
     devices,
     group,
-    audio,
-    w_enc,
-    table_span,
-    table_across,
-    bias,
-    intra_query,
-    intra_kv,
-    intra_out,
-    intra_up,
-    intra_down,
-    inter_query,
-    inter_kv,
-    inter_out,
-    inter_up,
-    inter_down,
-    enc_ref,
-    summed_ref,
-    samples,
+    *refs,
+):
+    given, refs = refs[:OPERANDS], refs[OPERANDS:]
+    (enc_ref, summed_ref), refs = refs[:2], refs[2:]
+    held, refs = refs[:OPERANDS], refs[OPERANDS:]
+    audio = given[0]
+    samples, w_enc, table_span, table_across, *layers = held
+    intra, inter_weights = layers[:5], layers[5:]
+    (
     frames,
     sent,
     taken,
@@ -250,7 +258,8 @@
     out_recv,
     back_send,
     back_recv,
-):
+    load,
+    ) = refs
     me = lax.axis_index("span")
     width = w_enc.shape[1]
     rows = audio.shape[0]
@@ -263,11 +272,16 @@
     part = share // chunks
     halo_rows = samples.shape[0] - rows
 
+    loads = []
+    for index in range(OPERANDS):
+        target = samples.at[pl.ds(0, rows)] if index == 0 else held[index]
+        loads.append(pltpu.make_async_copy(given[index], target, load.at[index]))
+        loads[-1].start()
+
     barrier = pltpu.get_barrier_semaphore()
     for step in range(1, devices):
         other = lax.rem(me + step, devices)
         pl.semaphore_signal(barrier, inc=1, device_id={"span": other}, device_id_type=MESH)
-    samples[:rows] = audio[...]
     pl.semaphore_wait(barrier, devices - 1)
 
     halo = pltpu.make_async_remote_copy(
@@ -286,10 +300,15 @@
     lane = lax.broadcasted_iota(jnp.int32, (1, LANES), 1)
     slot = lax.broadcasted_iota(jnp.int32, (HOP, 1), 0) % per_row
     mine = lane // STRIDE == slot
+    for index in range(4):
+        loads[index].wait()
     w_low = jnp.concatenate([w_enc[:STRIDE]] * per_row, axis=0)
     w_high = jnp.concatenate([w_enc[STRIDE:]] * per_row, axis=0)
     w_both = jnp.concatenate([w_low, w_high], axis=0)
     step_rows = HOP // per_row
+
+    kind = [lax.broadcasted_iota(jnp.int32, (group, group), axis) // total for axis in (0, 1)]
+    bias = jnp.where(kind[0] == kind[1], 0.0, -1e30)
 
     def encode(hop):
         at = hop * step_rows
@@ -312,6 +331,9 @@
     for hop in range(spans - 1):
         encode(hop)
 
+    for index in range(4, 9):
+        loads[index].wait()
+
     def send_out(index, step):
         other = lax.rem(me + step, devices)
         return pltpu.make_async_remote_copy(
@@ -323,8 +345,8 @@
             device_id_type=MESH,
         )
 
-    def do_span(index, _):
-        @pl.when(index == spans - 2)
+    def do_spans(pair, _):
+        @pl.when(pair == spans // 2 - 1)
         def _():
             @pl.when(me < devices - 1)
             def _():
@@ -337,24 +359,29 @@
             encode(spans - 1)
             encode(spans)
 
-        at = pl.multiple_of(index * HOP, HOP)
-        start = round_rows(
-            frames[pl.ds(at, K), :].astype(jnp.float32) + table_span[...]
-        )
-        result = layer_rows(
-            start, K, None, intra_query, intra_kv, intra_out, intra_up, intra_down
-        ).astype(jnp.bfloat16)
-        sent[index] = result.reshape(K // HOP, HOP, width)
-        for step in range(1, devices):
-            send_out(index, step).start()
-        taken[me * spans + index] = sent[
-            index, :, pl.ds(pl.multiple_of(me * share, TILE), share), :
-        ]
+        starts = []
+        for side in range(2):
+            at = pl.multiple_of((2 * pair + side) * HOP, HOP)
+            starts.append(
+                round_rows(frames[pl.ds(at, K), :].astype(jnp.float32) + table_span[...])
+            )
+        result = layer_rows(jnp.concatenate(starts, axis=0), K, None, *intra)
+        result = result.astype(jnp.bfloat16)
+        for side in range(2):
+            index = 2 * pair + side
+            sent[index] = result[side * K : (side + 1) * K].reshape(K // HOP, HOP, width)
+            for step in range(1, devices):
+                send_out(index, step).start()
+            taken[me * spans + index] = sent[
+                index, :, pl.ds(pl.multiple_of(me * share, TILE), share), :
+            ]
         return 0
 
-    lax.fori_loop(0, spans, do_span, 0)
+    lax.fori_loop(0, spans // 2, do_spans, 0)
     enc_ref[...] = frames[:count]
 
+    for index in range(9, OPERANDS):
+        loads[index].wait()
     owned = 2 * share
 
     def place(index, source):
@@ -387,23 +414,19 @@
         )
 
     def do_chunk(chunk, _):
-        def do_half(half, _):
-            first = half * share + chunk * part
-            block = jnp.concatenate(
-                [strided(across, first + p, total, owned) for p in range(part)], axis=0
-            )
-            result = layer_rows(
-                block, group, bias[...], inter_query, inter_kv, inter_out, inter_up, inter_down
-            )
-            at = pl.multiple_of(first * total, part * total)
-            result = round_rows(result)
+        firsts = [half * share + chunk * part for half in range(2)]
+        block = jnp.concatenate(
+            [strided(across, first + p, total, owned) for first in firsts for p in range(part)],
+            axis=0,
+        )
+        result = round_rows(layer_rows(block, group, bias, *inter_weights))
+        size = part * total
+        for half, first in enumerate(firsts):
+            at = pl.multiple_of(first * total, size)
             for side in range(width // LANES):
-                inter[side, pl.ds(at, part * total), :] = result[
-                    :, side * LANES : (side + 1) * LANES
+                inter[side, pl.ds(at, size), :] = result[
+                    half * size : (half + 1) * size, side * LANES : (side + 1) * LANES
                 ]
-            return 0
-
-        lax.fori_loop(0, 2, do_half, 0)
         near = chunk * part * total
         far = (share + chunk * part) * total
         pieces = []
@@ -465,17 +488,15 @@
     part = share // chunks
     group = LANES
     halo_rows = 2 * HOP * STRIDE // LANES
-    kind = np.arange(group) // total
-    bias = np.where(kind[:, None] == kind[None, :], 0.0, -1e30).astype(np.float32)
     operands = (
         audio.reshape(rows, LANES),
         w_enc,
         position_values(K, width),
         position_values(total, width),
-        bias,
         *layers,
     )
     vmem = pl.BlockSpec(memory_space=pltpu.VMEM)
+    far = pl.BlockSpec(memory_space=pl.ANY)
     dma = pltpu.SemaphoreType.DMA
     enc, summed = pl.pallas_call(
         functools.partial(separator_kernel, devices, group),
@@ -483,10 +504,11 @@
             jax.ShapeDtypeStruct((count, width), jnp.bfloat16),
             jax.ShapeDtypeStruct((spans, HOP, width), jnp.bfloat16),
         ],
-        in_specs=[vmem] * len(operands),
+        in_specs=[far] * len(operands),
         out_specs=[vmem] * 2,
         scratch_shapes=[
             pltpu.VMEM((rows + halo_rows, LANES), jnp.float32),
+            *[pltpu.VMEM(operand.shape, operand.dtype) for operand in operands[1:]],
             pltpu.VMEM((count + HOP, width), jnp.bfloat16),
             pltpu.VMEM((spans, K // HOP, HOP, width), jnp.bfloat16),
             pltpu.VMEM((total, K // HOP, share, width), jnp.bfloat16),
@@ -500,9 +522,10 @@
             dma((spans, devices)),
             dma((chunks, devices)),
             dma((chunks, devices)),
+            dma((len(operands),)),
         ],
         compiler_params=pltpu.CompilerParams(
-            collective_id=0, has_side_effects=True, vmem_limit_bytes=40 * 2**20
+            collective_id=0, has_side_effects=True, vmem_limit_bytes=60 * 2**20
         ),
     )(*operands)
     summed = summed.reshape(count, width)
@@ -518,7 +541,8 @@
         HOP % devices == 0
         and share % TILE == 0
         and LANES % (spans * devices) == 0
-        and spans >= 3
+        and spans >= 4
+        and spans % 2 == 0
         and devices > 1
     )
 

time: 55 us -> 38.1 us (0.69)
  local copies, waits for them, and re-layouts: 13.7 us -> 0.01 us
  Pallas kernels: 39.5 us -> 35.7 us
  matrix products: 1.1 us -> 2.21 us
    unnamed x32 -> x2, local copies, waits for them, and re-layouts: 13.7 us -> 0.01 us
    pallas_call x1, Pallas kernels: 39.5 us -> 35.7 us  [kernel_body(): pl.pallas_call(functools.partial(separator_kernel, devices, group), out_s...]
    dot_general x1, matrix products: 1.1 us -> 2.21 us  [kernel_body(): jnp.dot(summed, w_mask, preferred_element_type=jnp.float32)]
where the time goes in v2:
time: 38.1 us; the launch traced here: 38 us
  Pallas kernels  35.7 us (94%)
  matrix products  2.21 us (6%)
    pallas_call x1, Pallas kernels, kernel_body(): pl.pallas_call(functools.partial(separator_kernel, devices, group), out_s...  35.7 us
    dot_general x1, matrix products, kernel_body(): jnp.dot(summed, w_mask, preferred_element_type=jnp.float32)  2.21 us

profile of v2, /device:TPU:0, one launch (start us, length us, event | category | flops | bytes accessed | tf_op | source)
XLA Modules:
  0.0 38.0 jit_solution(331407324145669628)
XLA Ops:
  0.0 0.0 copy-start
  0.0 35.7 %shard_map.145 = (bf16[512,256]{1,0:T(8,128)(2,1)}, bf16[4,128,256]{2,1,0:T(8,128)(2,1)}) custom-call(f32[32,128]{1,0:T(8,128)} %bitcast.4, f32[16,256]{1,0:T(8,128)} %refs_1_.1, f32[256,256]{1,0:T(8,128)} %constant.7.clone.refs_2_, f32[32,256]{1,0:T(8,128)} %constant.8.clone.refs_3_, bf16[256,256]{1,0:T(8,128)(2,1)} %refs_4_.1, bf16[256,512]{1,0:T(8,128)(2,1)} %refs_5_.1, ...), custom_call_target="tpu_custom_call" | custom-call | tf_op jit(solution)/shard_map/pallas_call | solution.py:501
  35.8 0.0 copy-done
  35.8 2.2 %fusion.1 = bf16[512,512]{1,0:T(8,128)(2,1)} fusion(bf16[512,256]{1,0:T(8,128)(2,1)} %bitcast.5, bf16[256,512]{1,0:T(8,128)(2,1)S(1)} %copy-done, bf16[512,256]{1,0:T(8,128)(2,1)} %get-tuple-element.8), kind=kOutput, calls=%fused_computation.2 | convolution fusion | flops 136052736 | bytes 1310720 | tf_op jit(solution)/shard_map/dot_general | solution.py:532
Async XLA Ops:
  0.0 35.8 %copy-start = (bf16[256,512]{1,0:T(8,128)(2,1)S(1)}, bf16[256,512]{1,0:T(8,128)(2,1)}, u32[]{:S(2)}) copy-start(bf16[256,512]{1,0:T(8,128)(2,1)} %param.27) | copy-start | bytes 786436

commit v3 on v2

--- a/solution.py
+++ b/solution.py
@@ -211,11 +211,53 @@
     return jnp.concatenate(sides, axis=1).astype(jnp.bfloat16)
 
 
+def attend_few(query, key, value):
+    rows, width = query.shape
+    depth = width // HEADS
+    owner = lax.broadcasted_iota(jnp.int32, (1, LANES), 1) // depth
+    zero = jnp.zeros((), jnp.bfloat16)
+    ones = jnp.ones((key.shape[0], LANES), jnp.bfloat16)
+    heads = LANES // depth
+    sides = []
+    for at in range(0, width, LANES):
+        side_query, side_key, side_value = (
+            block[:, at : at + LANES] for block in (query, key, value)
+        )
+        scores = lax.dot_general(
+            jnp.concatenate(
+                [jnp.where(owner == head, side_query, zero) for head in range(heads)], axis=0
+            ),
+            side_key,
+            (((1,), (1,)), ((), ())),
+            preferred_element_type=jnp.float32,
+        )
+        scores = scores - jnp.max(scores, axis=-1, keepdims=True)
+        weights = jnp.exp2(scores.astype(jnp.bfloat16))
+        result = dot(weights, jnp.concatenate([side_value, ones], axis=1))
+        result = result[:, :LANES] / result[:, LANES:]
+        total = jnp.where(owner == 0, result[:rows], 0.0)
+        for head in range(1, heads):
+            total = jnp.where(owner == head, result[head * rows : (head + 1) * rows], total)
+        sides.append(total)
+    return jnp.concatenate(sides, axis=1).astype(jnp.bfloat16)
+
+
+def query_rows(normed, w_query):
+    scale = math.log2(math.e) / math.sqrt(normed.shape[1] // HEADS)
+    return (dot(normed, w_query[...]) * scale).astype(jnp.bfloat16)
+
+
+def rest_rows(rows, mixed, w_out, w_up, w_down):
+    middle = round_rows(rows + dot(mixed, w_out[...]))
+    second = norm_rows(middle).astype(jnp.bfloat16)
+    hidden = jnp.maximum(dot(second, w_up[...]), 0.0).astype(jnp.bfloat16)
+    return middle + dot(hidden, w_down[...])
+
+
 def layer_rows(rows, group, bias, w_query, w_kv, w_out, w_up, w_down):
     width = rows.shape[1]
     normed = norm_rows(rows).astype(jnp.bfloat16)
-    scale = math.log2(math.e) / math.sqrt(width // HEADS)
-    query = (dot(normed, w_query[...]) * scale).astype(jnp.bfloat16)
+    query = query_rows(normed, w_query)
     pair = dot(normed, w_kv[...]).astype(jnp.bfloat16)
     mixed = [
         attend_rows(
@@ -226,39 +268,31 @@
         )
         for at in range(0, rows.shape[0], group)
     ]
-    mixed = mixed[0] if len(mixed) == 1 else jnp.concatenate(mixed, axis=0)
-    middle = round_rows(rows + dot(mixed, w_out[...]))
-    second = norm_rows(middle).astype(jnp.bfloat16)
-    hidden = jnp.maximum(dot(second, w_up[...]), 0.0).astype(jnp.bfloat16)
-    return middle + dot(hidden, w_down[...])
-
-
-def separator_kernel(
-    devices,
-    group,
-    *refs,
-):
+    return rest_rows(rows, jnp.concatenate(mixed, axis=0), w_out, w_up, w_down)
+
+
+def separator_kernel(devices, group, *refs):
     given, refs = refs[:OPERANDS], refs[OPERANDS:]
     (enc_ref, summed_ref), refs = refs[:2], refs[2:]
     held, refs = refs[:OPERANDS], refs[OPERANDS:]
     audio = given[0]
     samples, w_enc, table_span, table_across, *layers = held
-    intra, inter_weights = layers[:5], layers[5:]
+    intra_query, intra_kv, *intra_rest = layers[:5]
+    inter_weights = layers[5:]
     (
-    frames,
-    sent,
-    taken,
-    across,
-    inter,
-    back,
-    got,
-    halo_send,
-    halo_recv,
-    out_send,
-    out_recv,
-    back_send,
-    back_recv,
-    load,
+        frames,
+        normed,
+        started,
+        mixed,
+        across,
+        inter,
+        back,
+        got,
+        audio_send,
+        audio_recv,
+        back_send,
+        back_recv,
+        load,
     ) = refs
     me = lax.axis_index("span")
     width = w_enc.shape[1]
@@ -267,14 +301,15 @@
     count = rows * per_row
     spans = count // HOP
     share = HOP // devices
+    owned = 2 * share
     total = spans * devices
     chunks = back.shape[0]
     part = share // chunks
-    halo_rows = samples.shape[0] - rows
-
+
+    own_rows = samples.at[pl.ds(pl.multiple_of(me * rows, rows), rows)]
     loads = []
     for index in range(OPERANDS):
-        target = samples.at[pl.ds(0, rows)] if index == 0 else held[index]
+        target = own_rows if index == 0 else held[index]
         loads.append(pltpu.make_async_copy(given[index], target, load.at[index]))
         loads[-1].start()
 
@@ -282,20 +317,22 @@
     for step in range(1, devices):
         other = lax.rem(me + step, devices)
         pl.semaphore_signal(barrier, inc=1, device_id={"span": other}, device_id_type=MESH)
+    ending = samples.shape[0] - rows * devices
+    samples[rows * devices :] = jnp.zeros((ending, LANES), jnp.float32)
     pl.semaphore_wait(barrier, devices - 1)
 
-    halo = pltpu.make_async_remote_copy(
-        src_ref=audio.at[pl.ds(0, halo_rows)],
-        dst_ref=samples.at[pl.ds(rows, halo_rows)],
-        send_sem=halo_send,
-        recv_sem=halo_recv,
-        device_id={"span": lax.rem(me + devices - 1, devices)},
-        device_id_type=MESH,
-    )
-
-    @pl.when(me > 0)
-    def _():
-        halo.start()
+    def send_audio(step):
+        return pltpu.make_async_remote_copy(
+            src_ref=audio,
+            dst_ref=own_rows,
+            send_sem=audio_send.at[step],
+            recv_sem=audio_recv.at[step],
+            device_id={"span": lax.rem(me + step, devices)},
+            device_id_type=MESH,
+        )
+
+    for step in (devices - 1, *range(1, devices - 1)):
+        send_audio(step).start()
 
     lane = lax.broadcasted_iota(jnp.int32, (1, LANES), 1)
     slot = lax.broadcasted_iota(jnp.int32, (HOP, 1), 0) % per_row
@@ -305,101 +342,101 @@
     w_low = jnp.concatenate([w_enc[:STRIDE]] * per_row, axis=0)
     w_high = jnp.concatenate([w_enc[STRIDE:]] * per_row, axis=0)
     w_both = jnp.concatenate([w_low, w_high], axis=0)
+    w_lead = w_both.astype(jnp.bfloat16)
+    w_rest = (w_both - w_lead.astype(jnp.float32)).astype(jnp.bfloat16)
     step_rows = HOP // per_row
-
     kind = [lax.broadcasted_iota(jnp.int32, (group, group), axis) // total for axis in (0, 1)]
     bias = jnp.where(kind[0] == kind[1], 0.0, -1e30)
 
     def encode(hop):
-        at = hop * step_rows
+        at = pl.multiple_of(hop * step_rows, step_rows)
         low = samples[pl.ds(at, step_rows), :]
         turned = pltpu.roll(samples[pl.ds(at, 2 * step_rows), :], LANES - STRIDE, 1)
         high = jnp.where(lane < LANES - STRIDE, turned[:step_rows], turned[1 : step_rows + 1])
-        spread = [
-            jnp.concatenate(
-                [jnp.broadcast_to(block[r : r + 1], (per_row, LANES)) for r in range(step_rows)],
-                axis=0,
-            )
-            for block in (low, high)
-        ]
-        picked = jnp.concatenate([jnp.where(mine, block, 0.0) for block in spread], axis=1)
-        result = jnp.dot(
-            picked, w_both, precision=lax.Precision.HIGHEST, preferred_element_type=jnp.float32
-        )
-        frames[pl.ds(hop * HOP, HOP), :] = jnp.maximum(result, 0.0).astype(jnp.bfloat16)
-
-    for hop in range(spans - 1):
-        encode(hop)
-
+        leads = []
+        rests = []
+        for block in (low, high):
+            lead = block.astype(jnp.bfloat16).astype(jnp.float32)
+            for values, into in ((lead, leads), (block - lead, rests)):
+                spread = jnp.concatenate(
+                    [
+                        jnp.broadcast_to(values[r : r + 1], (per_row, LANES))
+                        for r in range(step_rows)
+                    ],
+                    axis=0,
+                )
+                into.append(jnp.where(mine, spread, 0.0).astype(jnp.bfloat16))
+        lead = jnp.concatenate(leads, axis=1)
+        rest = jnp.concatenate(rests, axis=1)
+        result = dot(lead, w_lead) + (dot(rest, w_lead) + dot(lead, w_rest))
+        at = pl.multiple_of(hop * HOP, HOP)
+        frames[pl.ds(at, HOP), :] = jnp.maximum(result, 0.0).astype(jnp.bfloat16)
+
+    send_audio(devices - 1).wait_recv()
+    encode((me + 1) * spans)
     for index in range(4, 9):
         loads[index].wait()
-
-    def send_out(index, step):
-        other = lax.rem(me + step, devices)
-        return pltpu.make_async_remote_copy(
-            src_ref=sent.at[index, :, pl.ds(pl.multiple_of(other * share, TILE), share), :],
-            dst_ref=taken.at[me * spans + index],
-            send_sem=out_send.at[index, step],
-            recv_sem=out_recv.at[index, step],
-            device_id={"span": other},
-            device_id_type=MESH,
-        )
-
-    def do_spans(pair, _):
-        @pl.when(pair == spans // 2 - 1)
+    own = pl.multiple_of(me * share, TILE)
+
+    def attend_source(step, _):
+        @pl.when((step > 0) & (step < devices - 1))
         def _():
-            @pl.when(me < devices - 1)
-            def _():
-                halo.wait_recv()
-
-            @pl.when(me == devices - 1)
-            def _():
-                samples[rows:] = jnp.zeros((halo_rows, LANES), jnp.float32)
-
-            encode(spans - 1)
-            encode(spans)
-
-        starts = []
-        for side in range(2):
-            at = pl.multiple_of((2 * pair + side) * HOP, HOP)
-            starts.append(
-                round_rows(frames[pl.ds(at, K), :].astype(jnp.float32) + table_span[...])
+            send_audio(step).wait_recv()
+
+        source = lax.rem(me + devices - step, devices)
+        for index in range(spans):
+            encode(source * spans + index)
+        for index in range(spans):
+            span = source * spans + index
+            at = pl.multiple_of(span * HOP, HOP)
+            start = round_rows(frames[pl.ds(at, K), :].astype(jnp.float32) + table_span[...])
+            values = norm_rows(start).astype(jnp.bfloat16)
+            normed[index] = values.reshape(K // HOP, HOP, width)
+            for half in range(K // HOP):
+                at = pl.multiple_of(span * HOP + half * HOP + own, TILE)
+                table = table_span[pl.ds(pl.multiple_of(half * HOP + own, TILE), share), :]
+                value = round_rows(frames[pl.ds(at, share), :].astype(jnp.float32) + table)
+                at = pl.multiple_of(span * owned + half * share, TILE)
+                started[pl.ds(at, share), :] = value
+        pair = dot(normed[...].reshape(spans * K, width), intra_kv[...]).astype(jnp.bfloat16)
+        mine_normed = normed[:, :, pl.ds(own, share), :].reshape(spans * owned, width)
+        query = query_rows(mine_normed, intra_query)
+        values = [
+            attend_few(
+                query[index * owned : (index + 1) * owned],
+                pair[index * K : (index + 1) * K, :width],
+                pair[index * K : (index + 1) * K, width:],
             )
-        result = layer_rows(jnp.concatenate(starts, axis=0), K, None, *intra)
-        result = result.astype(jnp.bfloat16)
-        for side in range(2):
-            index = 2 * pair + side
-            sent[index] = result[side * K : (side + 1) * K].reshape(K // HOP, HOP, width)
-            for step in range(1, devices):
-                send_out(index, step).start()
-            taken[me * spans + index] = sent[
-                index, :, pl.ds(pl.multiple_of(me * share, TILE), share), :
+            for index in range(spans)
+        ]
+        at = pl.multiple_of(source * spans * owned, spans * owned)
+        mixed[pl.ds(at, spans * owned), :] = jnp.concatenate(values, axis=0)
+        return 0
+
+    lax.fori_loop(0, devices, attend_source, 0)
+    enc_ref[...] = frames[pl.ds(pl.multiple_of(me * count, count), count), :]
+
+    for index in range(9, OPERANDS):
+        loads[index].wait()
+    batch = total // 2
+
+    def finish_intra(half, _):
+        at = pl.multiple_of(half * batch * owned, batch * owned)
+        result = rest_rows(
+            started[pl.ds(at, batch * owned), :], mixed[pl.ds(at, batch * owned), :], *intra_rest
+        )
+        table = table_across[pl.ds(pl.multiple_of(half * batch, batch), batch), :]
+        table = jnp.concatenate(
+            [jnp.broadcast_to(table[c : c + 1], (owned, width)) for c in range(batch)], axis=0
+        )
+        result = round_rows(round_rows(result) + table)
+        for side in range(width // LANES):
+            across[side, pl.ds(at, batch * owned), :] = result[
+                :, side * LANES : (side + 1) * LANES
             ]
         return 0
 
-    lax.fori_loop(0, spans // 2, do_spans, 0)
-    enc_ref[...] = frames[:count]
-
-    for index in range(9, OPERANDS):
-        loads[index].wait()
-    owned = 2 * share
-
-    def place(index, source):
-        row = source * spans + index
-        block = taken[row].reshape(owned, width).astype(jnp.float32)
-        at = pl.multiple_of(row * owned, owned)
-        block = round_rows(block + table_across[pl.ds(row, 1), :])
-        for side in range(width // LANES):
-            across[side, pl.ds(at, owned), :] = block[:, side * LANES : (side + 1) * LANES]
-
-    def place_all(index, _):
-        place(index, me)
-        for step in range(1, devices):
-            send_out(index, step).wait_recv()
-            place(index, lax.rem(me + devices - step, devices))
-        return 0
-
-    lax.fori_loop(0, spans, place_all, 0)
+    lax.fori_loop(0, 2, finish_intra, 0)
 
     def send_back(chunk, step):
         other = lax.rem(me + step, devices)
@@ -458,21 +495,13 @@
             send_back(chunk, step).wait_recv()
         collect(lax.rem(me + devices - step, devices))
 
-    @pl.when(me > 0)
-    def _():
-        halo.wait_send()
-
-    def drain_out(index, _):
-        for step in range(1, devices):
-            send_out(index, step).wait_send()
-        return 0
-
     def drain_back(chunk, _):
         for step in range(1, devices):
             send_back(chunk, step).wait_send()
         return 0
 
-    lax.fori_loop(0, spans, drain_out, 0)
+    for step in range(1, devices):
+        send_audio(step).wait_send()
     lax.fori_loop(0, chunks, drain_back, 0)
 
 
@@ -487,7 +516,6 @@
     chunks = 2
     part = share // chunks
     group = LANES
-    halo_rows = 2 * HOP * STRIDE // LANES
     operands = (
         audio.reshape(rows, LANES),
         w_enc,
@@ -507,19 +535,18 @@
         in_specs=[far] * len(operands),
         out_specs=[vmem] * 2,
         scratch_shapes=[
-            pltpu.VMEM((rows + halo_rows, LANES), jnp.float32),
+            pltpu.VMEM((rows * devices + 2 * HOP * STRIDE // LANES, LANES), jnp.float32),
             *[pltpu.VMEM(operand.shape, operand.dtype) for operand in operands[1:]],
-            pltpu.VMEM((count + HOP, width), jnp.bfloat16),
+            pltpu.VMEM((total * HOP + HOP, width), jnp.bfloat16),
             pltpu.VMEM((spans, K // HOP, HOP, width), jnp.bfloat16),
-            pltpu.VMEM((total, K // HOP, share, width), jnp.bfloat16),
+            pltpu.VMEM((total * 2 * share, width), jnp.float32),
+            pltpu.VMEM((total * 2 * share, width), jnp.bfloat16),
             pltpu.VMEM((width // LANES, total * 2 * share, LANES), jnp.float32),
             pltpu.VMEM((width // LANES, total * 2 * share, LANES), jnp.float32),
             pltpu.VMEM((chunks, total * part, width), jnp.bfloat16),
             pltpu.VMEM((chunks, devices, spans * part, width), jnp.bfloat16),
-            dma,
-            dma,
-            dma((spans, devices)),
-            dma((spans, devices)),
+            dma((devices,)),
+            dma((devices,)),
             dma((chunks, devices)),
             dma((chunks, devices)),
             dma((len(operands),)),

time: 38.1 us -> 42.7 us (1.12)
  Pallas kernels: 35.7 us -> 40.4 us
    pallas_call x1, Pallas kernels: 35.7 us -> 40.4 us  [kernel_body(): pl.pallas_call(functools.partial(separator_kernel, devices, group), out_s...]
where the time goes in v3:
time: 42.7 us; the launch traced here: 42.6 us
  Pallas kernels  40.4 us (95%)
  matrix products  2.2 us (5%)
    pallas_call x1, Pallas kernels, kernel_body(): pl.pallas_call(functools.partial(separator_kernel, devices, group), out_s...  40.4 us
    dot_general x1, matrix products, kernel_body(): jnp.dot(summed, w_mask, preferred_element_type=jnp.float32)  2.2 us

profile of v3, /device:TPU:0, one launch (start us, length us, event | category | flops | bytes accessed | tf_op | source)
XLA Modules:
  0.0 42.6 jit_solution(4882360144540597916)
XLA Ops:
  0.0 0.0 copy-start
  0.0 40.4 %shard_map.145 = (bf16[512,256]{1,0:T(8,128)(2,1)}, bf16[4,128,256]{2,1,0:T(8,128)(2,1)}) custom-call(f32[32,128]{1,0:T(8,128)} %bitcast.4, f32[16,256]{1,0:T(8,128)} %refs_1_.1, f32[256,256]{1,0:T(8,128)} %constant.7.clone.refs_2_, f32[32,256]{1,0:T(8,128)} %constant.8.clone.refs_3_, bf16[256,256]{1,0:T(8,128)(2,1)} %refs_4_.1, bf16[256,512]{1,0:T(8,128)(2,1)} %refs_5_.1, ...), custom_call_target="tpu_custom_call" | custom-call | tf_op jit(solution)/shard_map/pallas_call | solution.py:529
  40.4 0.0 copy-done
  40.4 2.2 %fusion.1 = bf16[512,512]{1,0:T(8,128)(2,1)} fusion(bf16[512,256]{1,0:T(8,128)(2,1)} %bitcast.5, bf16[256,512]{1,0:T(8,128)(2,1)S(1)} %copy-done, bf16[512,256]{1,0:T(8,128)(2,1)} %get-tuple-element.8), kind=kOutput, calls=%fused_computation.2 | convolution fusion | flops 136052736 | bytes 1310720 | tf_op jit(solution)/shard_map/dot_general | solution.py:559
Async XLA Ops:
  0.0 40.4 %copy-start = (bf16[256,512]{1,0:T(8,128)(2,1)S(1)}, bf16[256,512]{1,0:T(8,128)(2,1)}, u32[]{:S(2)}) copy-start(bf16[256,512]{1,0:T(8,128)(2,1)} %param.27) | copy-start | bytes 786436

commit v4 on v3

--- a/solution.py
+++ b/solution.py
@@ -148,7 +148,7 @@
 
 LANES = 128
 TILE = 16
-OPERANDS = 14
+OPERANDS = 15
 MESH = pl.DeviceIdType.MESH
 
 
@@ -173,45 +173,6 @@
 
 
 def attend_rows(query, key, value, bias):
-    rows, width = query.shape
-    depth = width // HEADS
-    owner = lax.broadcasted_iota(jnp.int32, (1, LANES), 1) // depth
-    zero = jnp.zeros((), jnp.bfloat16)
-    ones = jnp.ones((rows, LANES), jnp.bfloat16)
-    heads = LANES // depth
-    sides = []
-    for at in range(0, width, LANES):
-        side_query, side_key, side_value = (
-            block[:, at : at + LANES] for block in (query, key, value)
-        )
-        scores = lax.dot_general(
-            jnp.concatenate(
-                [jnp.where(owner == head, side_query, zero) for head in range(heads)], axis=0
-            ),
-            side_key,
-            (((1,), (1,)), ((), ())),
-            preferred_element_type=jnp.float32,
-        )
-        weights = []
-        values = []
-        for head in range(heads):
-            part = scores[head * rows : (head + 1) * rows]
-            if bias is not None:
-                part = part + bias
-            part = part - jnp.max(part, axis=-1, keepdims=True)
-            weights.append(jnp.exp2(part.astype(jnp.bfloat16)))
-            mine = owner == head
-            values.append(
-                jnp.concatenate(
-                    [jnp.where(mine, side_value, zero), jnp.where(mine, ones, zero)], axis=1
-                )
-            )
-        result = dot(jnp.concatenate(weights, axis=1), jnp.concatenate(values, axis=0))
-        sides.append(result[:, :LANES] / result[:, LANES:])
-    return jnp.concatenate(sides, axis=1).astype(jnp.bfloat16)
-
-
-def attend_few(query, key, value):
     rows, width = query.shape
     depth = width // HEADS
     owner = lax.broadcasted_iota(jnp.int32, (1, LANES), 1) // depth
@@ -231,14 +192,16 @@
             (((1,), (1,)), ((), ())),
             preferred_element_type=jnp.float32,
         )
+        if bias is not None:
+            scores = scores + jnp.concatenate([bias] * heads, axis=0)
         scores = scores - jnp.max(scores, axis=-1, keepdims=True)
         weights = jnp.exp2(scores.astype(jnp.bfloat16))
         result = dot(weights, jnp.concatenate([side_value, ones], axis=1))
-        result = result[:, :LANES] / result[:, LANES:]
-        total = jnp.where(owner == 0, result[:rows], 0.0)
+        owners = jnp.concatenate([owner, owner], axis=1)
+        total = result[:rows]
         for head in range(1, heads):
-            total = jnp.where(owner == head, result[head * rows : (head + 1) * rows], total)
-        sides.append(total)
+            total = jnp.where(owners == head, result[head * rows : (head + 1) * rows], total)
+        sides.append(total[:, :LANES] / total[:, LANES:])
     return jnp.concatenate(sides, axis=1).astype(jnp.bfloat16)
 
 
@@ -273,23 +236,28 @@
 
 def separator_kernel(devices, group, *refs):
     given, refs = refs[:OPERANDS], refs[OPERANDS:]
-    (enc_ref, summed_ref), refs = refs[:2], refs[2:]
+    out_ref, refs = refs[0], refs[1:]
     held, refs = refs[:OPERANDS], refs[OPERANDS:]
     audio = given[0]
     samples, w_enc, table_span, table_across, *layers = held
     intra_query, intra_kv, *intra_rest = layers[:5]
-    inter_weights = layers[5:]
+    inter_weights = layers[5:10]
+    w_mask = layers[10]
     (
         frames,
         normed,
-        started,
-        mixed,
+        sent,
+        taken,
         across,
         inter,
         back,
         got,
         audio_send,
         audio_recv,
+        halo_send,
+        halo_recv,
+        out_send,
+        out_recv,
         back_send,
         back_recv,
         load,
@@ -305,11 +273,16 @@
     total = spans * devices
     chunks = back.shape[0]
     part = share // chunks
-
-    own_rows = samples.at[pl.ds(pl.multiple_of(me * rows, rows), rows)]
+    members = devices // 2
+    half_hop = HOP // 2
+    halo_rows = samples.shape[1] - rows
+    partner = lax.rem(me + members, devices)
+    group_at = me // members
+    member = lax.rem(me, members)
+
     loads = []
     for index in range(OPERANDS):
-        target = own_rows if index == 0 else held[index]
+        target = samples.at[0, pl.ds(0, rows)] if index == 0 else held[index]
         loads.append(pltpu.make_async_copy(given[index], target, load.at[index]))
         loads[-1].start()
 
@@ -317,22 +290,26 @@
     for step in range(1, devices):
         other = lax.rem(me + step, devices)
         pl.semaphore_signal(barrier, inc=1, device_id={"span": other}, device_id_type=MESH)
-    ending = samples.shape[0] - rows * devices
-    samples[rows * devices :] = jnp.zeros((ending, LANES), jnp.float32)
-    pl.semaphore_wait(barrier, devices - 1)
-
-    def send_audio(step):
+
+    def send_halo(section):
+        other = lax.rem(me + devices - 1 + section * members, devices)
         return pltpu.make_async_remote_copy(
-            src_ref=audio,
-            dst_ref=own_rows,
-            send_sem=audio_send.at[step],
-            recv_sem=audio_recv.at[step],
-            device_id={"span": lax.rem(me + step, devices)},
+            src_ref=audio.at[pl.ds(0, halo_rows)],
+            dst_ref=samples.at[section, pl.ds(rows, halo_rows)],
+            send_sem=halo_send.at[section],
+            recv_sem=halo_recv.at[section],
+            device_id={"span": other},
             device_id_type=MESH,
         )
 
-    for step in (devices - 1, *range(1, devices - 1)):
-        send_audio(step).start()
+    send_audio = pltpu.make_async_remote_copy(
+        src_ref=audio,
+        dst_ref=samples.at[1, pl.ds(0, rows)],
+        send_sem=audio_send,
+        recv_sem=audio_recv,
+        device_id={"span": partner},
+        device_id_type=MESH,
+    )
 
     lane = lax.broadcasted_iota(jnp.int32, (1, LANES), 1)
     slot = lax.broadcasted_iota(jnp.int32, (HOP, 1), 0) % per_row
@@ -348,10 +325,10 @@
     kind = [lax.broadcasted_iota(jnp.int32, (group, group), axis) // total for axis in (0, 1)]
     bias = jnp.where(kind[0] == kind[1], 0.0, -1e30)
 
-    def encode(hop):
-        at = pl.multiple_of(hop * step_rows, step_rows)
-        low = samples[pl.ds(at, step_rows), :]
-        turned = pltpu.roll(samples[pl.ds(at, 2 * step_rows), :], LANES - STRIDE, 1)
+    def encode(section, hop):
+        at = hop * step_rows
+        low = samples[section, pl.ds(at, step_rows), :]
+        turned = pltpu.roll(samples[section, pl.ds(at, 2 * step_rows), :], LANES - STRIDE, 1)
         high = jnp.where(lane < LANES - STRIDE, turned[:step_rows], turned[1 : step_rows + 1])
         leads = []
         rests = []
@@ -369,74 +346,104 @@
         lead = jnp.concatenate(leads, axis=1)
         rest = jnp.concatenate(rests, axis=1)
         result = dot(lead, w_lead) + (dot(rest, w_lead) + dot(lead, w_rest))
-        at = pl.multiple_of(hop * HOP, HOP)
-        frames[pl.ds(at, HOP), :] = jnp.maximum(result, 0.0).astype(jnp.bfloat16)
-
-    send_audio(devices - 1).wait_recv()
-    encode((me + 1) * spans)
+        frames[section, pl.ds(hop * HOP, HOP), :] = jnp.maximum(result, 0.0).astype(jnp.bfloat16)
+
+    for hop in range(spans - 1):
+        encode(0, hop)
+    pl.semaphore_wait(barrier, devices - 1)
+    send_halo(0).start()
+    send_audio.start()
+    send_halo(1).start()
     for index in range(4, 9):
         loads[index].wait()
-    own = pl.multiple_of(me * share, TILE)
-
-    def attend_source(step, _):
-        @pl.when((step > 0) & (step < devices - 1))
+    near = pl.multiple_of(group_at * half_hop, half_hop)
+
+    def send_out(section, step):
+        other = lax.rem(member + step, members)
+        source = lax.rem(me + section * members, devices)
+        return pltpu.make_async_remote_copy(
+            src_ref=sent.at[section, :, :, pl.ds(pl.multiple_of(other * share, TILE), share), :],
+            dst_ref=taken.at[pl.ds(source * spans, spans)],
+            send_sem=out_send.at[section, step],
+            recv_sem=out_recv.at[section, step],
+            device_id={"span": group_at * members + other},
+            device_id_type=MESH,
+        )
+
+    def do_section(section, _):
+        source = lax.rem(me + section * members, devices)
+
+        @pl.when(section == 1)
         def _():
-            send_audio(step).wait_recv()
-
-        source = lax.rem(me + devices - step, devices)
+            send_audio.wait_recv()
+            for hop in range(spans - 1):
+                encode(1, hop)
+
+        send_halo(section).wait_recv()
+
+        @pl.when(source == devices - 1)
+        def _():
+            samples[section, rows:] = jnp.zeros((halo_rows, LANES), jnp.float32)
+
+        encode(section, spans - 1)
+        encode(section, spans)
+        starts = []
         for index in range(spans):
-            encode(source * spans + index)
-        for index in range(spans):
-            span = source * spans + index
-            at = pl.multiple_of(span * HOP, HOP)
-            start = round_rows(frames[pl.ds(at, K), :].astype(jnp.float32) + table_span[...])
+            start = frames[section, pl.ds(index * HOP, K), :].astype(jnp.float32)
+            start = round_rows(start + table_span[...])
             values = norm_rows(start).astype(jnp.bfloat16)
             normed[index] = values.reshape(K // HOP, HOP, width)
             for half in range(K // HOP):
-                at = pl.multiple_of(span * HOP + half * HOP + own, TILE)
-                table = table_span[pl.ds(pl.multiple_of(half * HOP + own, TILE), share), :]
-                value = round_rows(frames[pl.ds(at, share), :].astype(jnp.float32) + table)
-                at = pl.multiple_of(span * owned + half * share, TILE)
-                started[pl.ds(at, share), :] = value
+                at = pl.multiple_of(index * HOP + half * HOP + near, half_hop)
+                start = frames[section, pl.ds(at, half_hop), :].astype(jnp.float32)
+                at = pl.multiple_of(half * HOP + near, half_hop)
+                starts.append(round_rows(start + table_span[pl.ds(at, half_hop), :]))
         pair = dot(normed[...].reshape(spans * K, width), intra_kv[...]).astype(jnp.bfloat16)
-        mine_normed = normed[:, :, pl.ds(own, share), :].reshape(spans * owned, width)
+        mine_normed = normed[:, :, pl.ds(near, half_hop), :].reshape(spans * HOP, width)
         query = query_rows(mine_normed, intra_query)
-        values = [
-            attend_few(
-                query[index * owned : (index + 1) * owned],
+        mixed = [
+            attend_rows(
+                query[index * HOP : (index + 1) * HOP],
                 pair[index * K : (index + 1) * K, :width],
                 pair[index * K : (index + 1) * K, width:],
+                None,
             )
             for index in range(spans)
         ]
-        at = pl.multiple_of(source * spans * owned, spans * owned)
-        mixed[pl.ds(at, spans * owned), :] = jnp.concatenate(values, axis=0)
+        result = rest_rows(
+            jnp.concatenate(starts, axis=0), jnp.concatenate(mixed, axis=0), *intra_rest
+        )
+        result = result.astype(jnp.bfloat16)
+        sent[section] = result.reshape(spans, K // HOP, half_hop, width)
+        for step in range(1, members):
+            send_out(section, step).start()
+        at = pl.multiple_of(member * share, TILE)
+        taken[pl.ds(source * spans, spans)] = sent[section, :, :, pl.ds(at, share), :]
         return 0
 
-    lax.fori_loop(0, devices, attend_source, 0)
-    enc_ref[...] = frames[pl.ds(pl.multiple_of(me * count, count), count), :]
+    lax.fori_loop(0, 2, do_section, 0)
 
     for index in range(9, OPERANDS):
         loads[index].wait()
-    batch = total // 2
-
-    def finish_intra(half, _):
-        at = pl.multiple_of(half * batch * owned, batch * owned)
-        result = rest_rows(
-            started[pl.ds(at, batch * owned), :], mixed[pl.ds(at, batch * owned), :], *intra_rest
-        )
-        table = table_across[pl.ds(pl.multiple_of(half * batch, batch), batch), :]
-        table = jnp.concatenate(
-            [jnp.broadcast_to(table[c : c + 1], (owned, width)) for c in range(batch)], axis=0
-        )
-        result = round_rows(round_rows(result) + table)
-        for side in range(width // LANES):
-            across[side, pl.ds(at, batch * owned), :] = result[
-                :, side * LANES : (side + 1) * LANES
-            ]
+
+    def place(source):
+        for index in range(spans):
+            row = source * spans + index
+            block = taken[row].reshape(owned, width).astype(jnp.float32)
+            at = pl.multiple_of(row * owned, owned)
+            block = round_rows(block + table_across[pl.ds(row, 1), :])
+            for side in range(width // LANES):
+                across[side, pl.ds(at, owned), :] = block[:, side * LANES : (side + 1) * LANES]
+
+    def place_section(section, _):
+        place(lax.rem(me + section * members, devices))
+        for step in range(1, members):
+            send_out(section, step).wait_recv()
+            other = group_at * members + lax.rem(member + members - step, members)
+            place(lax.rem(other + section * members, devices))
         return 0
 
-    lax.fori_loop(0, 2, finish_intra, 0)
+    lax.fori_loop(0, 2, place_section, 0)
 
     def send_back(chunk, step):
         other = lax.rem(me + step, devices)
@@ -486,8 +493,14 @@
             got[chunk, source].astype(jnp.float32).reshape(spans, part, width)
             for chunk in range(chunks)
         ]
+        summed = jnp.concatenate(pieces, axis=1).reshape(spans * share, width)
+        mask = jnp.maximum(dot(summed.astype(jnp.bfloat16), w_mask[...]), 0.0)
         at = pl.multiple_of(source * share, TILE)
-        summed_ref[:, pl.ds(at, share), :] = jnp.concatenate(pieces, axis=1).astype(jnp.bfloat16)
+        enc = [frames[0, pl.ds(span * HOP + at, share), :] for span in range(spans)]
+        enc = jnp.concatenate(enc, axis=0).astype(jnp.float32)
+        out = mask * jnp.concatenate([enc] * SPK, axis=1)
+        out = out.astype(jnp.bfloat16).reshape(spans, share, SPK * width)
+        out_ref[:, pl.ds(at, share), :] = out
 
     collect(me)
     for step in range(1, devices):
@@ -500,13 +513,15 @@
             send_back(chunk, step).wait_send()
         return 0
 
-    for step in range(1, devices):
-        send_audio(step).wait_send()
+    send_audio.wait_send()
+    for section in range(2):
+        send_halo(section).wait_send()
+        for step in range(1, members):
+            send_out(section, step).wait_send()
     lax.fori_loop(0, chunks, drain_back, 0)
 
 
 def kernel_body(devices, audio, w_enc, *weights):
-    *layers, w_mask = weights
     width = w_enc.shape[1]
     rows = audio.shape[0] // LANES
     count = audio.shape[0] // STRIDE
@@ -521,32 +536,33 @@
         w_enc,
         position_values(K, width),
         position_values(total, width),
-        *layers,
+        *weights,
     )
     vmem = pl.BlockSpec(memory_space=pltpu.VMEM)
     far = pl.BlockSpec(memory_space=pl.ANY)
     dma = pltpu.SemaphoreType.DMA
-    enc, summed = pl.pallas_call(
+    separated = pl.pallas_call(
         functools.partial(separator_kernel, devices, group),
-        out_shape=[
-            jax.ShapeDtypeStruct((count, width), jnp.bfloat16),
-            jax.ShapeDtypeStruct((spans, HOP, width), jnp.bfloat16),
-        ],
+        out_shape=jax.ShapeDtypeStruct((spans, HOP, SPK * width), jnp.bfloat16),
         in_specs=[far] * len(operands),
-        out_specs=[vmem] * 2,
+        out_specs=vmem,
         scratch_shapes=[
-            pltpu.VMEM((rows * devices + 2 * HOP * STRIDE // LANES, LANES), jnp.float32),
+            pltpu.VMEM((2, rows + 2 * HOP * STRIDE // LANES, LANES), jnp.float32),
             *[pltpu.VMEM(operand.shape, operand.dtype) for operand in operands[1:]],
-            pltpu.VMEM((total * HOP + HOP, width), jnp.bfloat16),
+            pltpu.VMEM((2, count + HOP, width), jnp.bfloat16),
             pltpu.VMEM((spans, K // HOP, HOP, width), jnp.bfloat16),
-            pltpu.VMEM((total * 2 * share, width), jnp.float32),
-            pltpu.VMEM((total * 2 * share, width), jnp.bfloat16),
+            pltpu.VMEM((2, spans, K // HOP, HOP // 2, width), jnp.bfloat16),
+            pltpu.VMEM((total, K // HOP, share, width), jnp.bfloat16),
             pltpu.VMEM((width // LANES, total * 2 * share, LANES), jnp.float32),
             pltpu.VMEM((width // LANES, total * 2 * share, LANES), jnp.float32),
             pltpu.VMEM((chunks, total * part, width), jnp.bfloat16),
             pltpu.VMEM((chunks, devices, spans * part, width), jnp.bfloat16),
-            dma((devices,)),
-            dma((devices,)),
+            dma,
+            dma,
+            dma((2,)),
+            dma((2,)),
+            dma((2, devices // 2)),
+            dma((2, devices // 2)),
             dma((chunks, devices)),
             dma((chunks, devices)),
             dma((len(operands),)),
@@ -555,10 +571,7 @@
             collective_id=0, has_side_effects=True, vmem_limit_bytes=60 * 2**20
         ),
     )(*operands)
-    summed = summed.reshape(count, width)
-    mask = jax.nn.relu(jnp.dot(summed, w_mask, preferred_element_type=jnp.float32))
-    repeated = jnp.concatenate([enc] * SPK, axis=1).astype(jnp.float32)
-    return (mask * repeated).astype(jnp.bfloat16)
+    return separated.reshape(count, SPK * width)
 
 
 def fits_kernel(devices, count):
@@ -568,9 +581,10 @@
         HOP % devices == 0
         and share % TILE == 0
         and LANES % (spans * devices) == 0
+        and share * (devices // 2) == HOP // 2
         and spans >= 4
         and spans % 2 == 0
-        and devices > 1
+        and devices % 2 == 0
     )
 
 

time: 42.7 us -> 37.8 us (0.89)
  Pallas kernels: 40.4 us -> 35.7 us
  matrix products: 2.2 us -> 0 us
  local copies, waits for them, and re-layouts: 0.01 us -> 1.87 us
    pallas_call x1, Pallas kernels: 40.4 us -> 35.7 us  [kernel_body(): pl.pallas_call(functools.partial(separator_kernel, devices, group), out_s...]
    dot_general x1 -> x0, matrix products: 2.2 us -> none  [kernel_body(): jnp.dot(summed, w_mask, preferred_element_type=jnp.float32)]
    unnamed x2 -> x1, local copies, waits for them, and re-layouts: 0.01 us -> 1.87 us
where the time goes in v4:
time: 37.8 us; the launch traced here: 37.5 us
  Pallas kernels  35.7 us (94%)
  local copies, waits for them, and re-layouts  1.87 us (5%)
    pallas_call x1, Pallas kernels, kernel_body(): pl.pallas_call(functools.partial(separator_kernel, devices, group), out_s...  35.7 us
    unnamed x1, local copies, waits for them, and re-layouts  1.87 us

profile of v4, /device:TPU:0, one launch (start us, length us, event | category | flops | bytes accessed | tf_op | source)
XLA Modules:
  0.0 37.5 jit_solution(180376059971676362)
XLA Ops:
  0.0 35.7 %shard_map.145 = bf16[4,128,512]{2,1,0:T(8,128)(2,1)} custom-call(f32[32,128]{1,0:T(8,128)} %bitcast.3, f32[16,256]{1,0:T(8,128)} %refs_1_.1, f32[256,256]{1,0:T(8,128)} %constant.4.clone.refs_2_, f32[32,256]{1,0:T(8,128)} %constant.5.clone.refs_3_, bf16[256,256]{1,0:T(8,128)(2,1)} %refs_4_.1, bf16[256,512]{1,0:T(8,128)(2,1)} %refs_5_.1, ...), custom_call_target="tpu_custom_call" | custom-call | tf_op jit(solution)/shard_map/pallas_call | solution.py:544
  35.7 1.9 %copy.17 = bf16[512,512]{1,0:T(8,128)(2,1)} copy(bf16[512,512]{1,0:T(8,128)(2,1)} %bitcast.2) | data formatting | bytes 1048576

commit v5 on v4

--- a/solution.py
+++ b/solution.py
@@ -163,6 +163,16 @@
     return jnp.dot(left, right, preferred_element_type=jnp.float32)
 
 
+def norm_wide(rows):
+    width = rows.shape[1]
+    ones = jnp.ones((width, LANES), jnp.bfloat16)
+    mean = dot(rows.astype(jnp.bfloat16), ones) * (1.0 / width)
+    center = [rows[:, at : at + LANES] - mean for at in range(0, width, LANES)]
+    squares = jnp.concatenate([(part * part).astype(jnp.bfloat16) for part in center], axis=1)
+    scale = lax.rsqrt(dot(squares, ones) * (1.0 / width) + 1e-05)
+    return jnp.concatenate([part * scale for part in center], axis=1)
+
+
 def round_rows(values):
     return values.astype(jnp.bfloat16).astype(jnp.float32)
 
@@ -212,14 +222,14 @@
 
 def rest_rows(rows, mixed, w_out, w_up, w_down):
     middle = round_rows(rows + dot(mixed, w_out[...]))
-    second = norm_rows(middle).astype(jnp.bfloat16)
+    second = norm_wide(middle).astype(jnp.bfloat16)
     hidden = jnp.maximum(dot(second, w_up[...]), 0.0).astype(jnp.bfloat16)
     return middle + dot(hidden, w_down[...])
 
 
 def layer_rows(rows, group, bias, w_query, w_kv, w_out, w_up, w_down):
     width = rows.shape[1]
-    normed = norm_rows(rows).astype(jnp.bfloat16)
+    normed = norm_wide(rows).astype(jnp.bfloat16)
     query = query_rows(normed, w_query)
     pair = dot(normed, w_kv[...]).astype(jnp.bfloat16)
     mixed = [
@@ -284,7 +294,8 @@
     for index in range(OPERANDS):
         target = samples.at[0, pl.ds(0, rows)] if index == 0 else held[index]
         loads.append(pltpu.make_async_copy(given[index], target, load.at[index]))
-        loads[-1].start()
+    for index in range(9):
+        loads[index].start()
 
     barrier = pltpu.get_barrier_semaphore()
     for step in range(1, devices):
@@ -356,6 +367,8 @@
     send_halo(1).start()
     for index in range(4, 9):
         loads[index].wait()
+    for index in range(9, OPERANDS):
+        loads[index].start()
     near = pl.multiple_of(group_at * half_hop, half_hop)
 
     def send_out(section, step):
@@ -391,7 +404,7 @@
         for index in range(spans):
             start = frames[section, pl.ds(index * HOP, K), :].astype(jnp.float32)
             start = round_rows(start + table_span[...])
-            values = norm_rows(start).astype(jnp.bfloat16)
+            values = norm_wide(start).astype(jnp.bfloat16)
             normed[index] = values.reshape(K // HOP, HOP, width)
             for half in range(K // HOP):
                 at = pl.multiple_of(index * HOP + half * HOP + near, half_hop)

time: 37.8 us -> 38.1 us (level)
  no operation moved by 1% of the time
where the time goes in v5:
time: 38.1 us; the launch traced here: 37.8 us
  Pallas kernels  36 us (94%)
  local copies, waits for them, and re-layouts  1.87 us (5%)
    pallas_call x1, Pallas kernels, kernel_body(): pl.pallas_call(functools.partial(separator_kernel, devices, group), out_s...  36 us
    unnamed x1, local copies, waits for them, and re-layouts  1.87 us

profile of v5, /device:TPU:0, one launch (start us, length us, event | category | flops | bytes accessed | tf_op | source)
XLA Modules:
  0.0 37.8 jit_solution(4883835455351778380)
XLA Ops:
  0.0 36.0 %shard_map.145 = bf16[4,128,512]{2,1,0:T(8,128)(2,1)} custom-call(f32[32,128]{1,0:T(8,128)} %bitcast.3, f32[16,256]{1,0:T(8,128)} %refs_1_.1, f32[256,256]{1,0:T(8,128)} %constant.4.clone.refs_2_, f32[32,256]{1,0:T(8,128)} %constant.5.clone.refs_3_, bf16[256,256]{1,0:T(8,128)(2,1)} %refs_4_.1, bf16[256,512]{1,0:T(8,128)(2,1)} %refs_5_.1, ...), custom_call_target="tpu_custom_call" | custom-call | tf_op jit(solution)/shard_map/pallas_call | solution.py:557
  36.0 1.9 %copy.17 = bf16[512,512]{1,0:T(8,128)(2,1)} copy(bf16[512,512]{1,0:T(8,128)(2,1)} %bitcast.2) | data formatting | bytes 1048576

commit v6 on v4

--- a/solution.py
+++ b/solution.py
@@ -217,23 +217,6 @@
     return middle + dot(hidden, w_down[...])
 
 
-def layer_rows(rows, group, bias, w_query, w_kv, w_out, w_up, w_down):
-    width = rows.shape[1]
-    normed = norm_rows(rows).astype(jnp.bfloat16)
-    query = query_rows(normed, w_query)
-    pair = dot(normed, w_kv[...]).astype(jnp.bfloat16)
-    mixed = [
-        attend_rows(
-            query[at : at + group],
-            pair[at : at + group, :width],
-            pair[at : at + group, width:],
-            bias,
-        )
-        for at in range(0, rows.shape[0], group)
-    ]
-    return rest_rows(rows, jnp.concatenate(mixed, axis=0), w_out, w_up, w_down)
-
-
 def separator_kernel(devices, group, *refs):
     given, refs = refs[:OPERANDS], refs[OPERANDS:]
     out_ref, refs = refs[0], refs[1:]
@@ -246,6 +229,10 @@
     (
         frames,
         normed,
+        started,
+        mixed,
+        queries,
+        pairs,
         sent,
         taken,
         across,
@@ -284,7 +271,8 @@
     for index in range(OPERANDS):
         target = samples.at[0, pl.ds(0, rows)] if index == 0 else held[index]
         loads.append(pltpu.make_async_copy(given[index], target, load.at[index]))
-        loads[-1].start()
+    for index in range(9):
+        loads[index].start()
 
     barrier = pltpu.get_barrier_semaphore()
     for step in range(1, devices):
@@ -326,7 +314,7 @@
     bias = jnp.where(kind[0] == kind[1], 0.0, -1e30)
 
     def encode(section, hop):
-        at = hop * step_rows
+        at = pl.multiple_of(hop * step_rows, step_rows)
         low = samples[section, pl.ds(at, step_rows), :]
         turned = pltpu.roll(samples[section, pl.ds(at, 2 * step_rows), :], LANES - STRIDE, 1)
         high = jnp.where(lane < LANES - STRIDE, turned[:step_rows], turned[1 : step_rows + 1])
@@ -346,16 +334,21 @@
         lead = jnp.concatenate(leads, axis=1)
         rest = jnp.concatenate(rests, axis=1)
         result = dot(lead, w_lead) + (dot(rest, w_lead) + dot(lead, w_rest))
-        frames[section, pl.ds(hop * HOP, HOP), :] = jnp.maximum(result, 0.0).astype(jnp.bfloat16)
-
-    for hop in range(spans - 1):
-        encode(0, hop)
+        at = pl.multiple_of(hop * HOP, HOP)
+        frames[section, pl.ds(at, HOP), :] = jnp.maximum(result, 0.0).astype(jnp.bfloat16)
+
+    def encode_all(section, first, last):
+        lax.fori_loop(first, last, lambda hop, _: (encode(section, hop), 0)[1], 0)
+
+    encode_all(0, 0, spans - 1)
     pl.semaphore_wait(barrier, devices - 1)
     send_halo(0).start()
     send_audio.start()
     send_halo(1).start()
     for index in range(4, 9):
         loads[index].wait()
+    for index in range(9, OPERANDS):
+        loads[index].start()
     near = pl.multiple_of(group_at * half_hop, half_hop)
 
     def send_out(section, step):
@@ -376,8 +369,6 @@
         @pl.when(section == 1)
         def _():
             send_audio.wait_recv()
-            for hop in range(spans - 1):
-                encode(1, hop)
 
         send_halo(section).wait_recv()
 
@@ -385,34 +376,30 @@
         def _():
             samples[section, rows:] = jnp.zeros((halo_rows, LANES), jnp.float32)
 
-        encode(section, spans - 1)
-        encode(section, spans)
-        starts = []
-        for index in range(spans):
-            start = frames[section, pl.ds(index * HOP, K), :].astype(jnp.float32)
+        encode_all(section, (spans - 1) * (1 - section), spans + 1)
+
+        def do_span(index, _):
+            at = pl.multiple_of(index * HOP, HOP)
+            start = frames[section, pl.ds(at, K), :].astype(jnp.float32)
             start = round_rows(start + table_span[...])
             values = norm_rows(start).astype(jnp.bfloat16)
-            normed[index] = values.reshape(K // HOP, HOP, width)
+            normed[...] = values.reshape(K // HOP, HOP, width)
             for half in range(K // HOP):
                 at = pl.multiple_of(index * HOP + half * HOP + near, half_hop)
                 start = frames[section, pl.ds(at, half_hop), :].astype(jnp.float32)
                 at = pl.multiple_of(half * HOP + near, half_hop)
-                starts.append(round_rows(start + table_span[pl.ds(at, half_hop), :]))
-        pair = dot(normed[...].reshape(spans * K, width), intra_kv[...]).astype(jnp.bfloat16)
-        mine_normed = normed[:, :, pl.ds(near, half_hop), :].reshape(spans * HOP, width)
-        query = query_rows(mine_normed, intra_query)
-        mixed = [
-            attend_rows(
-                query[index * HOP : (index + 1) * HOP],
-                pair[index * K : (index + 1) * K, :width],
-                pair[index * K : (index + 1) * K, width:],
-                None,
-            )
-            for index in range(spans)
-        ]
-        result = rest_rows(
-            jnp.concatenate(starts, axis=0), jnp.concatenate(mixed, axis=0), *intra_rest
-        )
+                start = round_rows(start + table_span[pl.ds(at, half_hop), :])
+                at = pl.multiple_of(index * HOP + half * half_hop, half_hop)
+                started[pl.ds(at, half_hop), :] = start
+            pair = dot(values, intra_kv[...]).astype(jnp.bfloat16)
+            mine_normed = normed[:, pl.ds(near, half_hop), :].reshape(HOP, width)
+            query = query_rows(mine_normed, intra_query)
+            at = pl.multiple_of(index * HOP, HOP)
+            mixed[pl.ds(at, HOP), :] = attend_rows(query, pair[:, :width], pair[:, width:], None)
+            return 0
+
+        lax.fori_loop(0, spans, do_span, 0)
+        result = rest_rows(started[...], mixed[...], *intra_rest)
         result = result.astype(jnp.bfloat16)
         sent[section] = result.reshape(spans, K // HOP, half_hop, width)
         for step in range(1, members):
@@ -427,13 +414,16 @@
         loads[index].wait()
 
     def place(source):
-        for index in range(spans):
+        def place_one(index, _):
             row = source * spans + index
             block = taken[row].reshape(owned, width).astype(jnp.float32)
             at = pl.multiple_of(row * owned, owned)
             block = round_rows(block + table_across[pl.ds(row, 1), :])
             for side in range(width // LANES):
                 across[side, pl.ds(at, owned), :] = block[:, side * LANES : (side + 1) * LANES]
+            return 0
+
+        lax.fori_loop(0, spans, place_one, 0)
 
     def place_section(section, _):
         place(lax.rem(me + section * members, devices))
@@ -463,7 +453,20 @@
             [strided(across, first + p, total, owned) for first in firsts for p in range(part)],
             axis=0,
         )
-        result = round_rows(layer_rows(block, group, bias, *inter_weights))
+        inter_query, inter_kv, *inter_rest = inter_weights
+        values = norm_rows(block).astype(jnp.bfloat16)
+        queries[...] = query_rows(values, inter_query)
+        pairs[...] = dot(values, inter_kv[...]).astype(jnp.bfloat16)
+
+        def do_group(index, _):
+            at = pl.ds(pl.multiple_of(index * group, group), group)
+            mixed[at, :] = attend_rows(
+                queries[at, :], pairs[at, :width], pairs[at, width:], bias
+            )
+            return 0
+
+        lax.fori_loop(0, 2 * part * total // group, do_group, 0)
+        result = round_rows(rest_rows(block, mixed[...], *inter_rest))
         size = part * total
         for half, first in enumerate(firsts):
             at = pl.multiple_of(first * total, size)
@@ -503,10 +506,14 @@
         out_ref[:, pl.ds(at, share), :] = out
 
     collect(me)
-    for step in range(1, devices):
+
+    def collect_step(step, _):
         for chunk in range(chunks):
             send_back(chunk, step).wait_recv()
         collect(lax.rem(me + devices - step, devices))
+        return 0
+
+    lax.fori_loop(1, devices, collect_step, 0)
 
     def drain_back(chunk, _):
         for step in range(1, devices):
@@ -550,7 +557,11 @@
             pltpu.VMEM((2, rows + 2 * HOP * STRIDE // LANES, LANES), jnp.float32),
             *[pltpu.VMEM(operand.shape, operand.dtype) for operand in operands[1:]],
             pltpu.VMEM((2, count + HOP, width), jnp.bfloat16),
-            pltpu.VMEM((spans, K // HOP, HOP, width), jnp.bfloat16),
+            pltpu.VMEM((K // HOP, HOP, width), jnp.bfloat16),
+            pltpu.VMEM((count, width), jnp.float32),
+            pltpu.VMEM((count, width), jnp.bfloat16),
+            pltpu.VMEM((count, width), jnp.bfloat16),
+            pltpu.VMEM((count, 2 * width), jnp.bfloat16),
             pltpu.VMEM((2, spans, K // HOP, HOP // 2, width), jnp.bfloat16),
             pltpu.VMEM((total, K // HOP, share, width), jnp.bfloat16),
             pltpu.VMEM((width // LANES, total * 2 * share, LANES), jnp.float32),
@@ -581,7 +592,6 @@
         HOP % devices == 0
         and share % TILE == 0
         and LANES % (spans * devices) == 0
-        and share * (devices // 2) == HOP // 2
         and spans >= 4
         and spans % 2 == 0
         and devices % 2 == 0

time: 37.8 us -> 45.4 us (1.20)
  Pallas kernels: 35.7 us -> 43.3 us
    pallas_call x1, Pallas kernels: 35.7 us -> 43.3 us  [kernel_body(): pl.pallas_call(functools.partial(separator_kernel, devices, group), out_s...]
where the time goes in v6:
time: 45.4 us; the launch traced here: 45.2 us
  Pallas kernels  43.3 us (95%)
  local copies, waits for them, and re-layouts  1.87 us (4%)
    pallas_call x1, Pallas kernels, kernel_body(): pl.pallas_call(functools.partial(separator_kernel, devices, group), out_s...  43.3 us
    unnamed x1, local copies, waits for them, and re-layouts  1.87 us

profile of v6, /device:TPU:0, one launch (start us, length us, event | category | flops | bytes accessed | tf_op | source)
XLA Modules:
  0.0 45.2 jit_solution(17335238505422222950)
XLA Ops:
  0.0 43.3 %shard_map.145 = bf16[4,128,512]{2,1,0:T(8,128)(2,1)} custom-call(f32[32,128]{1,0:T(8,128)} %bitcast.3, f32[16,256]{1,0:T(8,128)} %refs_1_.1, f32[256,256]{1,0:T(8,128)} %constant.4.clone.refs_2_, f32[32,256]{1,0:T(8,128)} %constant.5.clone.refs_3_, bf16[256,256]{1,0:T(8,128)(2,1)} %refs_4_.1, bf16[256,512]{1,0:T(8,128)(2,1)} %refs_5_.1, ...), custom_call_target="tpu_custom_call" | custom-call | tf_op jit(solution)/shard_map/pallas_call | solution.py:551
  43.3 1.9 %copy.17 = bf16[512,512]{1,0:T(8,128)(2,1)} copy(bf16[512,512]{1,0:T(8,128)(2,1)} %bitcast.2) | data formatting | bytes 1048576

commit v7 on v5

--- a/solution.py
+++ b/solution.py
@@ -150,6 +150,10 @@
 TILE = 16
 OPERANDS = 15
 MESH = pl.DeviceIdType.MESH
+
+
+def aligned(value, unit):
+    return value if isinstance(value, int) else pl.multiple_of(value, unit)
 
 
 def position_values(count, width):
@@ -369,13 +373,13 @@
         loads[index].wait()
     for index in range(9, OPERANDS):
         loads[index].start()
-    near = pl.multiple_of(group_at * half_hop, half_hop)
+    near = aligned(group_at * half_hop, half_hop)
 
     def send_out(section, step):
         other = lax.rem(member + step, members)
         source = lax.rem(me + section * members, devices)
         return pltpu.make_async_remote_copy(
-            src_ref=sent.at[section, :, :, pl.ds(pl.multiple_of(other * share, TILE), share), :],
+            src_ref=sent.at[section, :, :, pl.ds(aligned(other * share, TILE), share), :],
             dst_ref=taken.at[pl.ds(source * spans, spans)],
             send_sem=out_send.at[section, step],
             recv_sem=out_recv.at[section, step],
@@ -386,18 +390,15 @@
     def do_section(section, _):
         source = lax.rem(me + section * members, devices)
 
-        @pl.when(section == 1)
-        def _():
+        if section == 1:
             send_audio.wait_recv()
             for hop in range(spans - 1):
                 encode(1, hop)
 
         send_halo(section).wait_recv()
 
-        @pl.when(source == devices - 1)
-        def _():
-            samples[section, rows:] = jnp.zeros((halo_rows, LANES), jnp.float32)
-
+        halo = samples[section, rows:]
+        samples[section, rows:] = jnp.where(source == devices - 1, jnp.zeros_like(halo), halo)
         encode(section, spans - 1)
         encode(section, spans)
         starts = []
@@ -407,9 +408,9 @@
             values = norm_wide(start).astype(jnp.bfloat16)
             normed[index] = values.reshape(K // HOP, HOP, width)
             for half in range(K // HOP):
-                at = pl.multiple_of(index * HOP + half * HOP + near, half_hop)
+                at = aligned(index * HOP + half * HOP + near, half_hop)
                 start = frames[section, pl.ds(at, half_hop), :].astype(jnp.float32)
-                at = pl.multiple_of(half * HOP + near, half_hop)
+                at = aligned(half * HOP + near, half_hop)
                 starts.append(round_rows(start + table_span[pl.ds(at, half_hop), :]))
         pair = dot(normed[...].reshape(spans * K, width), intra_kv[...]).astype(jnp.bfloat16)
         mine_normed = normed[:, :, pl.ds(near, half_hop), :].reshape(spans * HOP, width)
@@ -430,11 +431,12 @@
         sent[section] = result.reshape(spans, K // HOP, half_hop, width)
         for step in range(1, members):
             send_out(section, step).start()
-        at = pl.multiple_of(member * share, TILE)
+        at = aligned(member * share, TILE)
         taken[pl.ds(source * spans, spans)] = sent[section, :, :, pl.ds(at, share), :]
         return 0
 
-    lax.fori_loop(0, 2, do_section, 0)
+    for section in range(2):
+        do_section(section, 0)
 
     for index in range(9, OPERANDS):
         loads[index].wait()
@@ -443,7 +445,7 @@
         for index in range(spans):
             row = source * spans + index
             block = taken[row].reshape(owned, width).astype(jnp.float32)
-            at = pl.multiple_of(row * owned, owned)
+            at = aligned(row * owned, owned)
             block = round_rows(block + table_across[pl.ds(row, 1), :])
             for side in range(width // LANES):
                 across[side, pl.ds(at, owned), :] = block[:, side * LANES : (side + 1) * LANES]
@@ -456,13 +458,14 @@
             place(lax.rem(other + section * members, devices))
         return 0
 
-    lax.fori_loop(0, 2, place_section, 0)
+    for section in range(2):
+        place_section(section, 0)
 
     def send_back(chunk, step):
         other = lax.rem(me + step, devices)
         size = spans * part
         return pltpu.make_async_remote_copy(
-            src_ref=back.at[chunk, pl.ds(pl.multiple_of(other * size, TILE), size), :],
+            src_ref=back.at[chunk, pl.ds(aligned(other * size, TILE), size), :],
             dst_ref=got.at[chunk, me],
             send_sem=back_send.at[chunk, step],
             recv_sem=back_recv.at[chunk, step],
@@ -479,7 +482,7 @@
         result = round_rows(layer_rows(block, group, bias, *inter_weights))
         size = part * total
         for half, first in enumerate(firsts):
-            at = pl.multiple_of(first * total, size)
+            at = aligned(first * total, size)
             for side in range(width // LANES):
                 inter[side, pl.ds(at, size), :] = result[
                     half * size : (half + 1) * size, side * LANES : (side + 1) * LANES
@@ -496,10 +499,11 @@
         for step in range(1, devices):
             send_back(chunk, step).start()
         size = spans * part
-        got[chunk, me] = back[chunk, pl.ds(pl.multiple_of(me * size, TILE), size), :]
+        got[chunk, me] = back[chunk, pl.ds(aligned(me * size, TILE), size), :]
         return 0
 
-    lax.fori_loop(0, chunks, do_chunk, 0)
+    for chunk in range(chunks):
+        do_chunk(chunk, 0)
 
     def collect(source):
         pieces = [
@@ -508,7 +512,7 @@
         ]
         summed = jnp.concatenate(pieces, axis=1).reshape(spans * share, width)
         mask = jnp.maximum(dot(summed.astype(jnp.bfloat16), w_mask[...]), 0.0)
-        at = pl.multiple_of(source * share, TILE)
+        at = aligned(source * share, TILE)
         enc = [frames[0, pl.ds(span * HOP + at, share), :] for span in range(spans)]
         enc = jnp.concatenate(enc, axis=0).astype(jnp.float32)
         out = mask * jnp.concatenate([enc] * SPK, axis=1)
@@ -531,7 +535,8 @@
         send_halo(section).wait_send()
         for step in range(1, members):
             send_out(section, step).wait_send()
-    lax.fori_loop(0, chunks, drain_back, 0)
+    for chunk in range(chunks):
+        drain_back(chunk, 0)
 
 
 def kernel_body(devices, audio, w_enc, *weights):

time: 38.1 us -> 38 us (level)
  no operation moved by 1% of the time
where the time goes in v7:
time: 38 us; the launch traced here: 37.8 us
  Pallas kernels  35.9 us (94%)
  local copies, waits for them, and re-layouts  1.87 us (5%)
    pallas_call x1, Pallas kernels, kernel_body(): pl.pallas_call(functools.partial(separator_kernel, devices, group), out_s...  35.9 us
    unnamed x1, local copies, waits for them, and re-layouts  1.87 us

profile of v7, /device:TPU:0, one launch (start us, length us, event | category | flops | bytes accessed | tf_op | source)
XLA Modules:
  0.0 37.8 jit_solution(1306135586614334809)
XLA Ops:
  0.0 35.9 %shard_map.145 = bf16[4,128,512]{2,1,0:T(8,128)(2,1)} custom-call(f32[32,128]{1,0:T(8,128)} %bitcast.3, f32[16,256]{1,0:T(8,128)} %refs_1_.1, f32[256,256]{1,0:T(8,128)} %constant.4.clone.refs_2_, f32[32,256]{1,0:T(8,128)} %constant.5.clone.refs_3_, bf16[256,256]{1,0:T(8,128)(2,1)} %refs_4_.1, bf16[256,512]{1,0:T(8,128)(2,1)} %refs_5_.1, ...), custom_call_target="tpu_custom_call" | custom-call | tf_op jit(solution)/shard_map/pallas_call | solution.py:562
  35.9 1.9 %copy.17 = bf16[512,512]{1,0:T(8,128)(2,1)} copy(bf16[512,512]{1,0:T(8,128)(2,1)} %bitcast.2) | data formatting | bytes 1048576
